TPU v7x, 32 devices: a whole 2x2x4 slice. The times are simulated.
32 devices in a mesh: outer: 2 (over x), inner: 4 (over z), tensor: 4 (over y, core).
Axes of the slice: x: 2, y: 2, z: 4, core: 2. Of those that a mesh axis runs over, the one named last changes fastest.
Arguments:
- queries: bfloat16 [2048, 16, 128], P(('outer', 'inner'), 'tensor'), may hold values from -5 to 5
- keys: bfloat16 [2048, 4, 128], P(('outer', 'inner'), 'tensor'), may hold values from -5 to 5
- values: bfloat16 [2048, 4, 128], P(('outer', 'inner'), 'tensor'), may hold values from -6 to 6
- w_out: bfloat16 [16, 128, 4096], P('tensor'), may hold values from -0.125 to 0.125
- d_out: bfloat16 [2048, 4096], P(('outer', 'inner', 'tensor')), may hold values from -6 to 6
- lengths: int32 [16], replicated, may hold values from 1 to 1280, 2048 in all
Outputs:
- mixed: bfloat16 [2048, 4096], P(('outer', 'inner', 'tensor'))
- d_queries: bfloat16 [2048, 16, 128], P(('outer', 'inner'), 'tensor')
- d_keys: bfloat16 [2048, 4, 128], P(('outer', 'inner'), 'tensor')
- d_values: bfloat16 [2048, 4, 128], P(('outer', 'inner'), 'tensor')
Inputs may be any that keep to these rules, and one draw needn't show every extreme that they name: `lengths`: the 16 documents fill the sequence of 2048 tokens exactly, and the longest has exactly 1280 tokens.
All inputs are finite; a program needn't handle non-finite values.
Results may differ from a plain program's by a relative error of at most 0.04.
Values may be sent and summed in bfloat16 or wider, within the bound.
No kernel may reach another device: no remote copies, remote signals or barrier semaphores. Data moves between devices by JAX's collectives and lax.ppermute only.
A program may use at most 128 MiB of HBM per device.

v0:
```python
import jax
import jax.numpy as jnp
from jax import lax
from jax.sharding import PartitionSpec as P

NEG_FILL = -1e30


def segment_of(positions, ends):
    return jnp.sum((positions[:, None] >= ends[None, :]).astype(jnp.int32), axis=1)


def doc_begin(position, ends):
    return jnp.max(jnp.where(ends <= position, ends, jnp.zeros_like(ends)))


def masked_scores(q_rows, k_block, q_pos, q_seg, k_start, ends, scale):
    width = k_block.shape[0]
    k_pos = k_start + jnp.arange(width, dtype=jnp.int32)
    k_seg = segment_of(k_pos, ends)
    s = (
        lax.dot_general(
            q_rows, k_block, (((1,), (1,)), ((), ())), preferred_element_type=jnp.float32
        )
        * scale
    )
    mask = (k_pos[None, :] <= q_pos[:, None]) & (k_seg[None, :] == q_seg[:, None])
    return (jnp.where(mask, s, NEG_FILL), mask)


def local(queries, keys, values, w_out, d_out, lengths):
    tok, heads_here, head_dim = queries.shape
    kv_here = keys.shape[1]
    group = heads_here // kv_here
    width = w_out.shape[2]
    ctx = lax.axis_size(("outer", "inner"))
    total = tok * ctx
    scale = head_dim ** (-0.5)
    offset = lax.axis_index(("outer", "inner")) * tok
    ends = jnp.cumsum(lengths)
    first = doc_begin(offset, ends)
    last = offset + tok - 1
    factor = 1
    while factor < ctx and tok * factor < 1024 and (ctx % (factor * 2) == 0):
        factor = factor * 2
    span = tok * factor
    n_blocks = total // span
    q_pos = offset + jnp.arange(tok * group, dtype=jnp.int32) // group
    q_seg = segment_of(q_pos, ends)
    key_all, value_all = (
        lax.all_gather(keys, ("outer", "inner"), axis=0, tiled=True),
        lax.all_gather(values, ("outer", "inner"), axis=0, tiled=True),
    )
    q_groups = queries.reshape(tok, kv_here, group, head_dim)
    zero = jnp.zeros((), jnp.int32)

    def needed(k_start, k_width):
        return (k_start <= last) & (k_start + k_width - 1 >= first)

    q_list = [q_groups[:, 0].reshape(tok * group, head_dim)]
    lse_list = []
    c = 0
    q_rows = q_list[c]

    def forward_block(b, carry, q_rows=q_rows, c=c):
        k_start = b * span

        def forward_work(state):
            top, denom, acc = state
            k_block = lax.dynamic_slice_in_dim(key_all, k_start, span, 0)[:, c]
            v_block = lax.dynamic_slice_in_dim(value_all, k_start, span, 0)[:, c]
            s, mask = masked_scores(q_rows, k_block, q_pos, q_seg, k_start, ends, scale)
            new_top = jnp.maximum(top, jnp.max(s, axis=1))
            weights = jnp.where(mask, jnp.exp(s - new_top[:, None]), 0.0)
            shrink = jnp.exp(top - new_top)
            denom = denom * shrink + jnp.sum(weights, axis=1)
            acc = acc * shrink[:, None] + jnp.dot(
                weights.astype(jnp.bfloat16), v_block, preferred_element_type=jnp.float32
            )
            return (new_top, denom, acc)

        return lax.cond(needed(k_start, span), forward_work, lambda st: st, carry)

    start_state = (
        jnp.full((tok * group,), NEG_FILL, jnp.float32),
        jnp.zeros((tok * group,), jnp.float32),
        jnp.zeros((tok * group, head_dim), jnp.float32),
    )
    top, denom, acc = lax.fori_loop(0, n_blocks, forward_block, start_state)
    attn_parts = [(acc / denom[:, None]).astype(jnp.bfloat16).reshape(tok, group, head_dim)]
    lse_list.append(top + jnp.log(denom))
    attn = jnp.stack(attn_parts, axis=1).reshape(tok, heads_here * head_dim)
    w_flat = w_out.reshape(heads_here * head_dim, width)
    mixed = lax.psum_scatter(
        jnp.dot(attn, w_flat, preferred_element_type=jnp.float32).astype(jnp.bfloat16),
        "tensor",
        scatter_dimension=0,
        tiled=True,
    )
    d_attn = lax.dot_general(
        lax.all_gather(d_out, "tensor", axis=0, tiled=True),
        w_flat,
        (((1,), (1,)), ((), ())),
        preferred_element_type=jnp.float32,
    ).astype(jnp.bfloat16)
    d_groups = d_attn.reshape(tok, kv_here, group, head_dim)
    a_groups = attn.reshape(tok, kv_here, group, head_dim)
    deltas = jnp.sum(d_groups.astype(jnp.float32) * a_groups.astype(jnp.float32), axis=3)
    g_list = [d_groups[:, 0].reshape(tok * group, head_dim)]
    delta_list = [deltas[:, 0].reshape(tok * group)]

    def grad_terms(c, k_start, k_width):
        k_block = lax.dynamic_slice_in_dim(key_all, k_start, k_width, 0)[:, c]
        v_block = lax.dynamic_slice_in_dim(value_all, k_start, k_width, 0)[:, c]
        s, mask = masked_scores(q_list[c], k_block, q_pos, q_seg, k_start, ends, scale)
        probs = jnp.where(mask, jnp.exp(s - lse_list[c][:, None]), 0.0)
        d_val = lax.dot_general(
            probs.astype(jnp.bfloat16),
            g_list[c],
            (((0,), (0,)), ((), ())),
            preferred_element_type=jnp.float32,
        )
        d_prob = lax.dot_general(
            g_list[c], v_block, (((1,), (1,)), ((), ())), preferred_element_type=jnp.float32
        )
        d_score = (probs * (d_prob - delta_list[c][:, None])).astype(jnp.bfloat16)
        dq_add = jnp.dot(d_score, k_block, preferred_element_type=jnp.float32) * scale
        d_key = (
            lax.dot_general(
                d_score, q_list[c], (((0,), (0,)), ((), ())), preferred_element_type=jnp.float32
            )
            * scale
        )
        return (dq_add, d_key, d_val)

    dq_start = tuple((jnp.zeros((tok * group, head_dim), jnp.float32) for c in range(kv_here)))

    def backward_block(b, carry):
        k_start = b * span

        def backward_work(state):
            dq_all, key_terms = state
            dq_add, d_key, d_val = grad_terms(0, k_start, span)
            new_dq = [dq_all[0] + dq_add]
            piece = jnp.stack((d_key, d_val), axis=1)[:, :, None, :]
            key_terms = lax.dynamic_update_slice(key_terms, piece, (k_start, zero, zero + 0, zero))
            return (tuple(new_dq), key_terms)

        return lax.cond(needed(k_start, span), backward_work, lambda st: st, carry)

    term_start = jnp.zeros((total, 2, kv_here, head_dim), jnp.float32)
    dq_all, key_terms = lax.fori_loop(0, n_blocks, backward_block, (dq_start, term_start))
    n_outer = lax.axis_size("outer")
    outer_terms = key_terms.reshape(n_outer, total // n_outer, 2, kv_here, head_dim)
    partial_value = lax.psum_scatter(
        outer_terms.astype(jnp.bfloat16), "outer", scatter_dimension=0, tiled=True
    ).astype(jnp.float32)
    partial_value = partial_value.reshape(total // n_outer, 2, kv_here, head_dim)
    key_grads = lax.psum_scatter(
        partial_value.astype(jnp.bfloat16), "inner", scatter_dimension=0, tiled=True
    ).astype(jnp.float32)
    d_queries = (
        jnp.stack([d.reshape(tok, group, head_dim) for d in dq_all], axis=1)
        .reshape(tok, heads_here, head_dim)
        .astype(jnp.bfloat16)
    )
    d_keys = key_grads[:, 0].astype(jnp.bfloat16)
    d_values = key_grads[:, 1].astype(jnp.bfloat16)
    return (mixed, d_queries, d_keys, d_values)


def solution(mesh):
    return jax.shard_map(
        local,
        mesh=mesh,
        in_specs=(
            P(("outer", "inner"), "tensor", None),
            P(("outer", "inner"), "tensor", None),
            P(("outer", "inner"), "tensor", None),
            P("tensor", None, None),
            P(("outer", "inner", "tensor"), None),
            P(),
        ),
        out_specs=(
            P(("outer", "inner", "tensor"), None),
            P(("outer", "inner"), "tensor", None),
            P(("outer", "inner"), "tensor", None),
            P(("outer", "inner"), "tensor", None),
        ),
        check_vma=False,
    )
```

profile of v0, /device:TPU:0, one launch (start us, length us, event | category | flops | bytes accessed | tf_op | source)
XLA Modules:
  0.0 213.5 jit_solution(14161848840215341540)
XLA Ops:
  7.2 0.7 all-gather.2.cloned.1.call-update
  7.9 0.7 copy.15
  8.9 0.6 fusion.57
  9.6 34.3 %all_gather.9 = bf16[2048,1,128]{2,0,1:T(8,128)(2,1)S(1)} all-gather(bf16[256,1,128]{2,0,1:T(8,128)(2,1)} %param.15), channel_id=1, replica_groups=mesh['outer'=2,'inner'=4,'tensor'=4] {'outer','inner'}, dimensions={0}, use_global_device_ids=true | all-gather | bytes 589824 | tf_op jit(solution)/shard_map/all_gather | solution.py:51
  43.9 32.5 %all_gather.10 = bf16[2048,1,128]{2,0,1:T(8,128)(2,1)S(1)} all-gather(bf16[256,1,128]{2,0,1:T(8,128)(2,1)} %param.16), channel_id=1, replica_groups=mesh['outer'=2,'inner'=4,'tensor'=4] {'outer','inner'}, dimensions={0}, use_global_device_ids=true | all-gather | bytes 589824 | tf_op jit(solution)/shard_map/all_gather | solution.py:52
  76.5 7.0 %while.42 = (s32[]{:T(128)}, f32[1024]{0:T(1024)S(1)}, f32[1024]{0:T(1024)S(1)}, f32[1024,128]{1,0:T(8,128)S(1)}, s32[]{:T(128)}, /*index=5*/s32[]{:T(128)}, s32...) while((s32[]{:T(128)}, f32[1024]{0:T(1024)S(1)}, ...), condition=%wide.region_9.10_spmd.clone, body=%wide.region_3.9_spmd.clone.sunk | while | flops 560262144 | bytes 14574053 | solution.py:89
  77.1 5.6 %conditional.6 = ((f32[1024]{0:T(1024)S(1)}, f32[1024]{0:T(1024)S(1)}, f32[1024,128]{1,0:T(8,128)S(1)})) conditional(s32[]{:T(128)} %convert_element_type.180, (f32[1024]{0:T(1024)S(1)}, f32[1024]{0:T(1024)S(1)}, f32[1024,128]{1,0:T(8,128)S(1)}) %tuple.137, (s32[]{:T(128)}, s32[]{:T(128)}, s32[16]{0:T(128)S(1)}, s32[1024]{0:T(1024)S(1)}, ...), branch_computations={%region_4.4_spmd, %region_5.8_spmd.clone} | conditional | flops 560261120 | bytes 14565526 | solution.py:82
  77.2 2.0 fusion.4
  79.3 1.6 fusion.6
  80.9 1.8 fusion.9
  83.4 0.6 log_add_fusion
  84.0 0.2 divide_convert_fusion
  84.3 4.1 %convolution_convert_fusion.1 = bf16[256,512]{1,0:T(8,128)(2,1)S(1)} fusion(bf16[256,4096]{1,0:T(8,128)(2,1)} %all-gather.2.cloned.1.call-done, bf16[512,4096]{1,0:T(8,128)(2,1)} %bitcast.108), kind=kOutput, calls=%fused_computation.67 | convolution fusion | flops 1073872896 | bytes 6553600 | tf_op jit(solution)/shard_map/dot_general | solution.py:100
  88.6 0.2 reshape.169
  88.8 0.4 fusion.52
  89.3 8.2 %while.43 = (s32[]{:T(128)}, f32[1024,128]{1,0:T(8,128)S(1)}, bf16[2048,2,1,128]{3,0,1,2:T(8,128)(2,1)S(1)}, s32[]{:T(128)}, s32[]{:T(128)}, /*index=5*/s32[16]{...) while((s32[]{:T(128)}, f32[1024,128]{1,0:T(8,128)S(1)}, ...), condition=%wide.region_16.17_spmd.clone, body=%wide.region_12.16_spmd.clone.sunk | while | flops 1362682880 | bytes 23441944 | solution.py:152
  90.0 6.8 %conditional.7 = ((f32[1024,128]{1,0:T(8,128)S(1)}, bf16[2048,2,1,128]{3,0,1,2:T(8,128)(2,1)S(1)})) conditional(s32[]{:T(128)} %convert_element_type.181, (f32[1024,128]{1,0:T(8,128)S(1)}, bf16[2048,2,1,128]{3,0,1,2:T(8,128)(2,1)S(1)}) %tuple.140, (s32[]{:T(128)}, s32[]{:T(128)}, s32[16]{0:T(128)}, s32[1024]{0:T(1024)S(1)}, ...), branch_computations={%region_13.13_spmd, %region_14.15_spmd.clone} | conditional | flops 1362681856 | bytes 23433394 | solution.py:149
  90.1 0.7 convert_reduce_fusion.1
  90.8 0.7 fusion.39
  91.6 1.7 fusion.31
  93.3 1.9 fusion.24
  95.2 0.8 fusion.35
  96.0 0.7 fusion.34
  97.5 1.0 copy-done.1
  98.6 1.2 dynamic-slice
  99.9 49.9 %all-reduce.3.cloned.1.call-done = bf16[2,1024,2,1,128]{4,1,0,2,3:T(8,128)(2,1)} async-done(((bf16[2,1024,2,1,128]{4,1,0,2,3:T(8,128)(2,1)}), bf16[2,1024,2,1,128]{4,1,0,2,3:T(8,128)(2,1)}) %all-reduce.3.cloned.1.call-update) | async-done | bytes 1048592
  149.7 2.5 %dynamic-slice_bitcast_fusion = bf16[1024,2,1,128]{3,0,1,2:T(8,128)(2,1)} fusion(bf16[2,1024,2,1,128]{4,1,0,2,3:T(8,128)(2,1)} %all-reduce.3.cloned.1.call-done, u32[]{:T(128)} %bitcast.29), kind=kLoop, calls=%fused_computation.70 | loop fusion | bytes 1048580 | tf_op jit(solution)/shard_map/convert_element_type | solution.py:160
  152.5 4.8 %convolution_convert_fusion = bf16[256,4096]{1,0:T(8,128)(2,1)} fusion(bf16[256,512]{1,0:T(8,128)(2,1)S(1)} %reshape_stack_reshape.4, bf16[512,4096]{1,0:T(8,128)(2,1)} %bitcast.109), kind=kOutput, calls=%fused_computation.66 | convolution fusion | flops 1074790400 | bytes 6553600 | tf_op jit(solution)/shard_map/dot_general | solution.py:95
  157.3 0.7 convert_element_type.147
  158.0 16.0 %reduce-scatter.8.cloned.1.call-done = bf16[256,2,1,128]{3,0,1,2:T(8,128)(2,1)} async-done(((bf16[1024,2,1,128]{3,0,1,2:T(8,128)(2,1)}), bf16[256,2,1,128]{3,0,1,2:T(8,128)(2,1)}) %reduce-scatter.8.cloned.1.call-update) | async-done | bytes 131088 | tf_op jit(solution)/shard_map/reduce_scatter | solution.py:159
  174.1 1.5 slice_bitcast_fusion
  175.6 31.4 %reduce-scatter.6.cloned.1.call-done = bf16[64,4096]{1,0:T(8,128)(2,1)} async-done(((bf16[256,4096]{1,0:T(8,128)(2,1)}), bf16[64,4096]{1,0:T(8,128)(2,1)}) %reduce-scatter.6.cloned.1.call-update) | async-done | bytes 524304 | tf_op jit(solution)/shard_map/reduce_scatter | solution.py:94
  (44 shorter events, 1.3 us)
Async XLA Ops:
  7.2 77.1 %all-gather.2.cloned.1.call-start = ((), (), s32[]{:S(2)}) async-start(), calls=%async_computation.3 | async-start | bytes 2621440 | tf_op jit(solution)/shard_map/all_gather | solution.py:101
  7.9 141.8 %all-reduce.3.cloned.1.call-start = ((), (), s32[]{:S(2)}) async-start(), calls=%async_computation.5 | async-start | bytes 2097152
  83.4 5.0 %copy-start.2 = (s32[16]{0:T(128)}, s32[16]{0:T(128)S(1)}, u32[]{:S(2)}) copy-start(s32[16]{0:T(128)S(1)} %get-tuple-element.1467) | copy-start | bytes 196
  84.3 5.0 %copy-start = (bf16[1024,128]{1,0:T(8,128)(2,1)S(1)}, bf16[1024,128]{1,0:T(8,128)(2,1)}, u32[]{:S(2)}) copy-start(bf16[1024,128]{1,0:T(8,128)(2,1)} %get-tuple-element.1449) | copy-start | bytes 786436
  90.1 1.5 copy-start.3
  97.5 1.0 copy-start.1
  98.6 75.5 %reduce-scatter.8.cloned.1.call-start = ((), (), s32[]{:S(2)}) async-start(), calls=%async_computation.4 | async-start | bytes 655360 | tf_op jit(solution)/shard_map/reduce_scatter | solution.py:159
  152.3 54.7 %reduce-scatter.6.cloned.1.call-start = ((), (), s32[]{:S(2)}) async-start(), calls=%async_computation.2 | async-start | bytes 2621440 | tf_op jit(solution)/shard_map/reduce_scatter | solution.py:94
Sparse Core Ops, SparseCore 0:
  9.6 25.2 all-gather.1
  98.7 50.9 all-reduce.2
  152.4 21.6 reduce-scatter.7
  177.2 29.7 reduce-scatter.5
where the time goes:
time: 214 us; the launch traced here: 213 us
  waiting for transfers between devices  98 us (46%)
  blocking collectives  66.8 us (31%)
  matrix products  18.6 us (9%)
  between operations  13.9 us (6%)
  local copies, waits for them, and re-layouts  7.84 us (4%)
  other arithmetic  5.3 us (2%)
  loops' own time  2.87 us (1%)
    unnamed x5, waiting for transfers between devices  50.6 us
    all_gather x1, blocking collectives, local(): lax.all_gather(keys, ('outer', 'inner'), axis=0, tiled=True)  34.3 us
    all_gather x1, blocking collectives, local(): lax.all_gather(values, ('outer', 'inner'), axis=0, tiled=True)  32.5 us
    reduce_scatter x1, waiting for transfers between devices, local(): lax.psum_scatter(jnp.dot(attn, w_flat, preferred_element_type=jnp.float32...  31.4 us
    reduce_scatter x1, waiting for transfers between devices, local(): lax.psum_scatter(partial_value.astype(jnp.bfloat16), 'inner', scatter_dim...  16 us
    dot_general x1, matrix products, local(): jnp.dot(attn, w_flat, preferred_element_type=jnp.float32)  4.8 us
  transfers between devices with their start and end apart: 4, of which 3 were waited for; matrix products, arithmetic and copies ran while one was open for 8% of the time, Pallas kernels for 0%

commit v1 on v0

v1 whole, which is shorter than its diff:
```python
import functools

import jax
import jax.numpy as jnp
from jax import lax
from jax.experimental import pallas as pl
from jax.experimental.pallas import tpu as pltpu
from jax.sharding import PartitionSpec as P

NEG_FILL = -1e30
LOG2E = 1.4426950408889634
CTX = ("outer", "inner")
F32 = jnp.float32
BF16 = jnp.bfloat16


def dot_nt(a, b):
    return lax.dot_general(a, b, (((1,), (1,)), ((), ())), preferred_element_type=F32)


def dot_nn(a, b):
    return jnp.dot(a, b, preferred_element_type=F32)


def layout_of(len_ref, me, tok):
    offset = me * tok
    q_pos = offset + lax.broadcasted_iota(jnp.int32, (1, tok), 1)
    begin = jnp.zeros((1, tok), jnp.int32)
    first = jnp.int32(0)
    end = jnp.int32(0)
    for j in range(len_ref.shape[0]):
        end = end + len_ref[j]
        begin = jnp.where(q_pos >= end, end, begin)
        first = jnp.where(offset >= end, end, first)
    n_blocks = me - first // tok + 1
    return q_pos, begin, n_blocks


def bias_of(q_pos, begin, k_start, tok):
    k_pos = k_start + lax.broadcasted_iota(jnp.int32, (tok, tok), 0)
    return jnp.where((k_pos >= begin) & (k_pos <= q_pos), 0.0, NEG_FILL).astype(F32)


def forward_kernel(
    n_kv, heads, scale, len_ref, q_ref, *refs
):
    kv_refs = refs[:n_kv]
    own_ref, pair_ref, w_hbm = refs[n_kv : n_kv + 3]
    far_send, far_keep, near_send, near_keep, attn_ref, lse_ref, d_attn_ref = refs[n_kv + 3 : n_kv + 10]
    kvs, acc, top, denom, rows, w_vmem, w_sem = refs[n_kv + 10 :]
    tok = q_ref.shape[0]
    hd = q_ref.shape[1] // heads
    me = lax.axis_index(CTX)
    t = lax.axis_index("tensor")
    w_copy = pltpu.make_async_copy(w_hbm, w_vmem, w_sem)
    w_copy.start()
    q_pos, begin, n_blocks = layout_of(len_ref, me, tok)
    for d in range(n_kv):

        @pl.when(d < n_blocks)
        def _():
            kvs[d] = kv_refs[d][...]

    top[...] = jnp.full(top.shape, NEG_FILL, F32)
    denom[...] = jnp.zeros(denom.shape, F32)
    acc[...] = jnp.zeros(acc.shape, F32)

    def block(d, carry):
        k = kvs[d, :, :hd]
        v_t = kvs[d, :, hd:].T
        bias = bias_of(q_pos, begin, (me - d) * tok, tok)
        for h in range(heads):
            s = dot_nt(k, q_ref[:, h * hd : (h + 1) * hd]) * (scale * LOG2E) + bias
            old = top[h : h + 1, :]
            new = jnp.maximum(old, jnp.max(s, axis=0, keepdims=True))
            p = jnp.exp2(s - new)
            shrink = jnp.exp2(old - new)
            top[h : h + 1, :] = new
            denom[h : h + 1, :] = denom[h : h + 1, :] * shrink + jnp.sum(p, axis=0, keepdims=True)
            part = slice(h * hd, (h + 1) * hd)
            acc[part, :] = acc[part, :] * shrink + dot_nn(v_t, p.astype(BF16))
        return carry

    lax.fori_loop(0, n_blocks, block, 0)
    lse_ref[...] = top[...] + jnp.log(denom[...]) * LOG2E
    for h in range(heads):
        part = slice(h * hd, (h + 1) * hd)
        out = acc[part, :] / denom[h : h + 1, :]
        attn_ref[:, part] = out.T.astype(BF16)
    quarter = tok // 4
    for i, mask in enumerate((3, 2, 1, 0)):
        rows[i * quarter : (i + 1) * quarter, :] = attn_ref[pl.ds(pl.multiple_of((t ^ mask) * quarter, quarter), quarter), :]
    w_copy.wait()
    width = w_vmem.shape[1]
    step = 512
    for n in range(width // step):
        cols = slice(n * step, (n + 1) * step)
        mixed = dot_nn(rows[...], w_vmem[:, cols]).astype(BF16)
        for i, ref in enumerate((far_send, far_keep, near_send, near_keep)):
            ref[:, cols] = mixed[i * quarter : (i + 1) * quarter, :]
    core = t & 1
    d_attn_ref[pl.ds(pl.multiple_of(core * quarter, quarter), quarter), :] = dot_nt(own_ref[...], w_vmem[...]).astype(BF16)
    d_attn_ref[pl.ds(pl.multiple_of((1 - core) * quarter, quarter), quarter), :] = dot_nt(
        pair_ref[...], w_vmem[...]
    ).astype(BF16)


def backward_kernel(n_kv, heads, scale, len_ref, q_ref, *refs):
    kv_refs = refs[:n_kv]
    attn_ref, lse_ref, near_ref, cross_ref, diag_ref, w_hbm = refs[n_kv : n_kv + 6]
    dq_ref = refs[n_kv + 6]
    out_refs = refs[n_kv + 7 : 2 * n_kv + 7]
    kvs, terms, dq_t, delta, g, w_vmem, w_sem = refs[2 * n_kv + 7 :]
    tok = q_ref.shape[0]
    hd = q_ref.shape[1] // heads
    me = lax.axis_index(CTX)
    t = lax.axis_index("tensor")
    w_copy = pltpu.make_async_copy(w_hbm, w_vmem, w_sem)
    w_copy.start()
    q_pos, begin, n_blocks = layout_of(len_ref, me, tok)
    for d in range(n_kv):

        @pl.when(d < n_blocks)
        def _():
            kvs[d] = kv_refs[d][...]

    quarter = tok // 4
    half = tok // 2
    chip = t >> 1
    g[pl.ds(pl.multiple_of(chip * half, half), half), :] = near_ref[...]
    w_copy.wait()
    for mask, ref in ((2, cross_ref), (3, diag_ref)):
        g[pl.ds(pl.multiple_of((t ^ mask) * quarter, quarter), quarter), :] = dot_nt(ref[...], w_vmem[...]).astype(BF16)
    for h in range(heads):
        part = slice(h * hd, (h + 1) * hd)
        prod = g[:, part].astype(F32) * attn_ref[:, part].astype(F32)
        delta[h : h + 1, :] = jnp.sum(prod.T, axis=0, keepdims=True)
    dq_t[...] = jnp.zeros(dq_t.shape, F32)

    def block(d, carry):
        k = kvs[d, :, :hd]
        v = kvs[d, :, hd:]
        k_t = k.T
        bias = bias_of(q_pos, begin, (me - d) * tok, tok)
        dk = jnp.zeros((tok, hd), F32)
        dv = jnp.zeros((tok, hd), F32)
        for h in range(heads):
            part = slice(h * hd, (h + 1) * hd)
            q = q_ref[:, part]
            g_h = g[:, part]
            s = dot_nt(k, q) * (scale * LOG2E) + bias
            p = jnp.exp2(s - lse_ref[h : h + 1, :])
            dp = dot_nt(v, g_h)
            ds = (p * (dp - delta[h : h + 1, :])).astype(BF16)
            dv = dv + dot_nn(p.astype(BF16), g_h)
            dk = dk + dot_nn(ds, q)
            dq_t[part, :] = dq_t[part, :] + dot_nn(k_t, ds)
        terms[d, :, :hd] = dk * scale
        terms[d, :, hd:] = dv
        return carry

    lax.fori_loop(0, n_blocks, block, 0)
    out_refs[0][...] = terms[0]
    for d in range(1, n_kv):

        @pl.when(d < n_blocks)
        def _():
            out_refs[d][...] = terms[d].astype(BF16)

        @pl.when(d >= n_blocks)
        def _():
            out_refs[d][...] = jnp.zeros(out_refs[d].shape, BF16)

    for h in range(heads):
        part = slice(h * hd, (h + 1) * hd)
        dq_ref[:, part] = (dq_t[part, :] * scale).T.astype(BF16)


def local(queries, keys, values, w_out, d_out, lengths):
    tok, heads, hd = queries.shape
    width = w_out.shape[2]
    ctx = lax.axis_size(CTX)
    longest = tok * ctx * 5 // 8
    reach = min(ctx - 1, -(-(longest - 1) // tok))
    n_kv = reach + 1
    scale = hd ** (-0.5)
    quarter = tok // 4
    n_tensor = lax.axis_size("tensor")

    def swap(x, mask):
        return lax.ppermute(x, "tensor", [(i, i ^ mask) for i in range(n_tensor)])

    def shift(x, d):
        pairs = [(i, i + d) for i in range(ctx - d)] if d > 0 else [(i - d, i) for i in range(ctx + d)]
        return lax.ppermute(x, CTX, pairs)

    q = queries.reshape(tok, heads * hd)
    kv = jnp.concatenate([keys.reshape(tok, hd), values.reshape(tok, hd)], axis=1)
    cross = swap(d_out, 2)
    pair = swap(d_out, 1)
    kvs = [kv] + [shift(kv, d) for d in range(1, n_kv)]
    diag = swap(cross, 1)
    w = w_out.reshape(heads * hd, width)

    vmem = pl.BlockSpec(memory_space=pltpu.VMEM)
    smem = pl.BlockSpec(memory_space=pltpu.SMEM)
    hbm = pl.BlockSpec(memory_space=pl.ANY)
    row = jax.ShapeDtypeStruct((quarter, width), BF16)
    far_send, far_keep, near_send, near_keep, attn, lse, d_near = pl.pallas_call(
        functools.partial(forward_kernel, n_kv, heads, scale),
        out_shape=(
            row,
            row,
            row,
            row,
            jax.ShapeDtypeStruct((tok, heads * hd), BF16),
            jax.ShapeDtypeStruct((heads, tok), F32),
            jax.ShapeDtypeStruct((tok // 2, heads * hd), BF16),
        ),
        in_specs=[smem] + [vmem] * (n_kv + 3) + [hbm],
        out_specs=(vmem,) * 7,
        scratch_shapes=[
            pltpu.VMEM((n_kv, tok, 2 * hd), BF16),
            pltpu.VMEM((heads * hd, tok), F32),
            pltpu.VMEM((heads, tok), F32),
            pltpu.VMEM((heads, tok), F32),
            pltpu.VMEM((tok, heads * hd), BF16),
            pltpu.VMEM((heads * hd, width), BF16),
            pltpu.SemaphoreType.DMA(()),
        ],
        compiler_params=pltpu.CompilerParams(vmem_limit_bytes=40 * 2**20),
        name="forward",
    )(lengths, q, *kvs, d_out, pair, w)

    from_pair = swap(far_send, 1)
    to_cross = (from_pair.astype(F32) + far_keep.astype(F32)).astype(BF16)
    from_cross = swap(to_cross, 2)
    near_pair = swap(near_send, 1)

    dq, *terms = pl.pallas_call(
        functools.partial(backward_kernel, n_kv, heads, scale),
        out_shape=(
            jax.ShapeDtypeStruct((tok, heads * hd), BF16),
            jax.ShapeDtypeStruct((tok, 2 * hd), F32),
        )
        + (jax.ShapeDtypeStruct((tok, 2 * hd), BF16),) * reach,
        in_specs=[smem] + [vmem] * (n_kv + 6) + [hbm],
        out_specs=(vmem,) * (n_kv + 1),
        scratch_shapes=[
            pltpu.VMEM((n_kv, tok, 2 * hd), BF16),
            pltpu.VMEM((n_kv, tok, 2 * hd), F32),
            pltpu.VMEM((heads * hd, tok), F32),
            pltpu.VMEM((heads, tok), F32),
            pltpu.VMEM((tok, heads * hd), BF16),
            pltpu.VMEM((heads * hd, width), BF16),
            pltpu.SemaphoreType.DMA(()),
        ],
        compiler_params=pltpu.CompilerParams(vmem_limit_bytes=48 * 2**20),
        name="backward",
    )(lengths, q, *kvs, attn, lse, d_near, cross, diag, w)

    total = terms[0]
    for d in range(1, n_kv):
        total = total + shift(terms[d], -d).astype(F32)
    mixed = (near_keep.astype(F32) + near_pair.astype(F32) + from_cross.astype(F32)).astype(BF16)
    grads = total.astype(BF16).reshape(tok, 1, 2 * hd)
    return (mixed, dq.reshape(tok, heads, hd), grads[:, :, :hd], grads[:, :, hd:])


def solution(mesh):
    return jax.shard_map(
        local,
        mesh=mesh,
        in_specs=(
            P(("outer", "inner"), "tensor", None),
            P(("outer", "inner"), "tensor", None),
            P(("outer", "inner"), "tensor", None),
            P("tensor", None, None),
            P(("outer", "inner", "tensor"), None),
            P(),
        ),
        out_specs=(
            P(("outer", "inner", "tensor"), None),
            P(("outer", "inner"), "tensor", None),
            P(("outer", "inner"), "tensor", None),
            P(("outer", "inner"), "tensor", None),
        ),
        check_vma=False,
    )
```

time: 214 us -> 84.7 us (0.40)
  blocking collectives: 66.8 us -> 0 us
  waiting for transfers between devices: 98 us -> 32.4 us
  starting transfers between devices: 0.16 us -> 29.9 us
  matrix products: 18.6 us -> 0 us
  between operations: 13.9 us -> 0.86 us
  Pallas kernels: 0 us -> 13 us
  loops' own time: 2.87 us -> 0 us
    all_gather x2 -> x0, blocking collectives: 66.8 us -> none  [the longest x1 34.3 us: local(): lax.all_gather(keys, ('outer', 'inner'), axis=0, tiled=True)]
    unnamed x5 -> x0, waiting for transfers between devices: 50.6 us -> none
    reduce_scatter x2 -> x0, waiting for transfers between devices: 47.4 us -> none  [the longest x1 31.4 us: local(): lax.psum_scatter(jnp.dot(attn, w_flat, preferred_element_type=jnp.float32...]
    ppermute x0 -> x16, waiting for transfers between devices: none -> 32.4 us  [the longest x10 21.4 us: shift(): return lax.ppermute(x, CTX, pairs)]
    ppermute x0 -> x16, starting transfers between devices: none -> 29.9 us  [the longest x10 26.1 us: shift(): return lax.ppermute(x, CTX, pairs)]
    dot_general x9 -> x0, matrix products: 18.6 us -> none  [the longest x1 4.8 us: local(): jnp.dot(attn, w_flat, preferred_element_type=jnp.float32)]
    pallas_call x0 -> x2, Pallas kernels: none -> 13 us  [the longest x1 6.95 us: local(): pl.pallas_call(functools.partial(backward_kernel, n_kv, heads, scale), ou...]
    convert_element_type x3 -> x0, local copies, waits for them, and re-layouts: 4.22 us -> none  [the longest x1 2.52 us: local(): partial_value.astype(jnp.bfloat16)]
  transfers between devices with their start and end apart: 4 -> 16, of which waited for: 3 -> 3; matrix products, arithmetic and copies ran while one was open for 8% -> 5% of each run, Pallas kernels for 0% -> 15%
where the time goes in v1:
time: 84.7 us; the launch traced here: 85.8 us
  waiting for transfers between devices  32.4 us (38%)
  starting transfers between devices  29.9 us (35%)
  Pallas kernels  13 us (15%)
  local copies, waits for them, and re-layouts  6.4 us (8%)
  other arithmetic  3.25 us (4%)
  between operations  0.86 us (1%)
    ppermute x10, starting transfers between devices, shift(): return lax.ppermute(x, CTX, pairs)  26.1 us
    ppermute x10, waiting for transfers between devices, shift(): return lax.ppermute(x, CTX, pairs)  21.4 us
    ppermute x6, waiting for transfers between devices, swap(): return lax.ppermute(x, 'tensor', [(i, i ^ mask) for i in range(n_tensor)])  11 us
    pallas_call x1, Pallas kernels, local(): pl.pallas_call(functools.partial(backward_kernel, n_kv, heads, scale), ou...  6.95 us
    pallas_call x1, Pallas kernels, local(): pl.pallas_call(functools.partial(forward_kernel, n_kv, heads, scale), out...  6.08 us
    unnamed x13, local copies, waits for them, and re-layouts  4.98 us
    ppermute x6, starting transfers between devices, swap(): return lax.ppermute(x, 'tensor', [(i, i ^ mask) for i in range(n_tensor)])  3.75 us
  transfers between devices with their start and end apart: 16, of which 3 were waited for; matrix products, arithmetic and copies ran while one was open for 5% of the time, Pallas kernels for 15%

profile of v1, /device:TPU:0, one launch (start us, length us, event | category | flops | bytes accessed | tf_op | source)
XLA Modules:
  0.0 85.8 jit_solution(12574123396548756655)
XLA Ops:
  0.6 0.0 copy-start.3
  0.6 3.0 %collective-permute-start.9 = (bf16[64,4096]{1,0:T(8,128)(2,1)}, bf16[64,4096]{1,0:T(8,128)(2,1)S(1)}, u32[]{:S(2)}, u32[]{:S(2)}) collective-permute-start(bf16[64,4096]{1,0:T(8,128)(2,1)} %refs_6_.1), channel_id=1, source_target_pairs={{0,2},{1,3},{2,0},{3,1},{4,6},{5,7},{6,4},{7,5},{8,10},{9,11},{10,... | collective-permute-start | bytes 1572872 | tf_op jit(solution)/shard_map/ppermute | solution.py:191
  3.7 0.9 %pad_maximum_fusion.refs_0_ = bf16[256,256]{1,0:T(8,128)(2,1)S(1)} fusion(bf16[256,128]{1,0:T(8,128)(2,1)} %bitcast.14, bf16[256,128]{1,0:T(8,128)(2,1)} %bitcast.15), kind=kLoop, calls=%fused_computation.5 | loop fusion | flops 262144 | bytes 262144 | tf_op jit(solution)/shard_map/concatenate | solution.py:198
  4.6 3.5 %collective-permute-start = (bf16[256,256]{1,0:T(8,128)(2,1)S(1)}, bf16[256,256]{1,0:T(8,128)(2,1)S(1)}, u32[]{:S(2)}, u32[]{:S(2)}) collective-permute-start(bf16[256,256]{1,0:T(8,128)(2,1)S(1)} %pad_maximum_fusion.refs_0_), channel_id=1, source_target_pairs={{0,4},{4,8},{8,12},{12,16},{16,20},{20,24},{24,28},{1,5},{5,9},{9,... | collective-permute-start | bytes 393224 | tf_op jit(solution)/shard_map/ppermute | solution.py:195
  8.1 4.5 %collective-permute-start.1 = (bf16[256,256]{1,0:T(8,128)(2,1)S(1)}, bf16[256,256]{1,0:T(8,128)(2,1)S(1)}, u32[]{:S(2)}, u32[]{:S(2)}) collective-permute-start(bf16[256,256]{1,0:T(8,128)(2,1)S(1)} %pad_maximum_fusion.refs_0_), channel_id=1, source_target_pairs={{0,8},{4,12},{8,16},{12,20},{16,24},{20,28},{1,9},{5,13},{9,17},{1... | collective-permute-start | bytes 393224 | tf_op jit(solution)/shard_map/ppermute | solution.py:195
  12.6 4.2 %collective-permute-start.2 = (bf16[256,256]{1,0:T(8,128)(2,1)S(1)}, bf16[256,256]{1,0:T(8,128)(2,1)S(1)}, u32[]{:S(2)}, u32[]{:S(2)}) collective-permute-start(bf16[256,256]{1,0:T(8,128)(2,1)S(1)} %pad_maximum_fusion.refs_0_), channel_id=1, source_target_pairs={{0,12},{4,16},{8,20},{12,24},{16,28},{1,13},{5,17},{9,21},{13,25},... | collective-permute-start | bytes 393224 | tf_op jit(solution)/shard_map/ppermute | solution.py:195
  16.8 1.7 %collective-permute-start.3 = (bf16[256,256]{1,0:T(8,128)(2,1)S(1)}, bf16[256,256]{1,0:T(8,128)(2,1)S(1)}, u32[]{:S(2)}, u32[]{:S(2)}) collective-permute-start(bf16[256,256]{1,0:T(8,128)(2,1)S(1)} %pad_maximum_fusion.refs_0_), channel_id=1, source_target_pairs={{0,16},{4,20},{8,24},{12,28},{1,17},{5,21},{9,25},{13,29},{2,18},{... | collective-permute-start | bytes 393224 | tf_op jit(solution)/shard_map/ppermute | solution.py:195
  18.5 5.8 %collective-permute-start.4 = (bf16[256,256]{1,0:T(8,128)(2,1)S(1)}, bf16[256,256]{1,0:T(8,128)(2,1)S(1)}, u32[]{:S(2)}, u32[]{:S(2)}) collective-permute-start(bf16[256,256]{1,0:T(8,128)(2,1)S(1)} %pad_maximum_fusion.refs_0_), channel_id=1, source_target_pairs={{0,20},{4,24},{8,28},{1,21},{5,25},{9,29},{2,22},{6,26},{10,30},{3... | collective-permute-start | bytes 393224 | tf_op jit(solution)/shard_map/ppermute | solution.py:195
  24.3 0.1 collective-permute-start.10
  24.4 1.0 %copy.12 = bf16[32,8,4,128]{3,1,2,0:T(8,128)(2,1)S(1)} copy(bf16[32,8,4,128]{3,2,1,0:T(4,128)(2,1)} %bitcast.13) | data formatting | bytes 524288
  25.4 1.5 %collective-permute-done.4.refs_5_ = bf16[256,256]{1,0:T(8,128)(2,1)S(1)} collective-permute-done((bf16[256,256]{1,0:T(8,128)(2,1)S(1)}, bf16[256,256]{1,0:T(8,128)(2,1)S(1)}, u32[]{:S(2)}, u32[]{:S(2)}) %collective-permute-start.4) | collective-permute-done | bytes 131104 | tf_op jit(solution)/shard_map/ppermute | solution.py:195
  26.9 2.2 %copy-done = bf16[4,128,4096]{2,1,0:T(8,128)(2,1)S(1)} copy-done((bf16[4,128,4096]{2,1,0:T(8,128)(2,1)S(1)}, bf16[4,128,4096]{2,1,0:T(8,128)(2,1)}, u32[]{:S(2)}) %copy-start) | copy-done | bytes 4194328
  29.1 1.0 %copy-done.1 = bf16[64,4096]{1,0:T(8,128)(2,1)S(1)} copy-done((bf16[64,4096]{1,0:T(8,128)(2,1)S(1)}, bf16[64,4096]{1,0:T(8,128)(2,1)}, u32[]{:S(2)}) %copy-start.1) | copy-done | bytes 524312
  30.2 0.7 copy-done.2
  30.8 6.1 %forward.1 = (bf16[64,4096]{1,0:T(8,128)(2,1)S(1)}, bf16[64,4096]{1,0:T(8,128)(2,1)S(1)}, bf16[64,4096]{1,0:T(8,128)(2,1)S(1)}, bf16[64,4096]{1,0:T(8,128)(2,1)S...) custom-call(s32[16]{0:T(128)S(1)} %copy-done.2, ...), custom_call_target="tpu_custom_call" | custom-call | tf_op jit(solution)/shard_map/forward/pallas_call | solution.py:209
  36.9 0.1 collective-permute-start.7
  37.0 7.0 %backward.1 = (bf16[256,512]{1,0:T(8,128)(2,1)S(1)}, f32[256,256]{1,0:T(8,128)S(1)}, bf16[256,256]{1,0:T(8,128)(2,1)S(1)}, bf16[256,256]{1,0:T(8,128)(2,1)S(1)},...) custom-call(s32[16]{0:T(128)S(1)} %copy-done.3, ...), custom_call_target="tpu_custom_call" | custom-call | tf_op jit(solution)/shard_map/backward/pallas_call | solution.py:240
  44.0 1.3 %collective-permute-start.15 = (bf16[256,256]{1,0:T(8,128)(2,1)S(1)}, bf16[256,256]{1,0:T(8,128)(2,1)S(1)}, u32[]{:S(2)}, u32[]{:S(2)}) collective-permute-start(bf16[256,256]{1,0:T(8,128)(2,1)S(1)} %get-tuple-element.31), channel_id=1, source_target_pairs={{20,0},{24,4},{28,8},{21,1},{25,5},{29,9},{22,2},{26,6},{30,10},{2... | collective-permute-start | bytes 393224 | tf_op jit(solution)/shard_map/ppermute | solution.py:195
  45.3 1.3 %collective-permute-start.14 = (bf16[256,256]{1,0:T(8,128)(2,1)S(1)}, bf16[256,256]{1,0:T(8,128)(2,1)S(1)}, u32[]{:S(2)}, u32[]{:S(2)}) collective-permute-start(bf16[256,256]{1,0:T(8,128)(2,1)S(1)} %get-tuple-element.30), channel_id=1, source_target_pairs={{16,0},{20,4},{24,8},{28,12},{17,1},{21,5},{25,9},{29,13},{18,2},{... | collective-permute-start | bytes 393224 | tf_op jit(solution)/shard_map/ppermute | solution.py:195
  46.6 1.3 %collective-permute-start.13 = (bf16[256,256]{1,0:T(8,128)(2,1)S(1)}, bf16[256,256]{1,0:T(8,128)(2,1)}, u32[]{:S(2)}, u32[]{:S(2)}) collective-permute-start(bf16[256,256]{1,0:T(8,128)(2,1)S(1)} %get-tuple-element.29), channel_id=1, source_target_pairs={{12,0},{16,4},{20,8},{24,12},{28,16},{13,1},{17,5},{21,9},{25,13},... | collective-permute-start | bytes 393224 | tf_op jit(solution)/shard_map/ppermute | solution.py:195
  47.9 1.3 %collective-permute-start.12 = (bf16[256,256]{1,0:T(8,128)(2,1)S(1)}, bf16[256,256]{1,0:T(8,128)(2,1)}, u32[]{:S(2)}, u32[]{:S(2)}) collective-permute-start(bf16[256,256]{1,0:T(8,128)(2,1)S(1)} %get-tuple-element.28), channel_id=1, source_target_pairs={{8,0},{12,4},{16,8},{20,12},{24,16},{28,20},{9,1},{13,5},{17,9},{2... | collective-permute-start | bytes 393224 | tf_op jit(solution)/shard_map/ppermute | solution.py:195
  49.2 1.3 %collective-permute-start.11 = (bf16[256,256]{1,0:T(8,128)(2,1)S(1)}, bf16[256,256]{1,0:T(8,128)(2,1)}, u32[]{:S(2)}, u32[]{:S(2)}) collective-permute-start(bf16[256,256]{1,0:T(8,128)(2,1)S(1)} %get-tuple-element.27), channel_id=1, source_target_pairs={{4,0},{8,4},{12,8},{16,12},{20,16},{24,20},{28,24},{5,1},{9,5},{13... | collective-permute-start | bytes 393224 | tf_op jit(solution)/shard_map/ppermute | solution.py:195
  50.5 0.1 add_convert_fusion.1
  50.6 19.9 %collective-permute-done.15 = bf16[256,256]{1,0:T(8,128)(2,1)S(1)} collective-permute-done((bf16[256,256]{1,0:T(8,128)(2,1)S(1)}, bf16[256,256]{1,0:T(8,128)(2,1)S(1)}, u32[]{:S(2)}, u32[]{:S(2)}) %collective-permute-start.15) | collective-permute-done | bytes 131104 | tf_op jit(solution)/shard_map/ppermute | solution.py:195
  70.5 0.6 collective-permute-start.8
  71.1 0.1 copy-done.4
  71.1 0.0 copy-done.5
  71.2 0.8 reshape.30
  71.9 1.3 %fusion = bf16[256,1,256]{2,0,1:T(8,128)(2,1)S(1)} fusion(bf16[256,256]{1,0:T(8,128)(2,1)} %copy-done.4, bf16[256,256]{1,0:T(8,128)(2,1)} %copy-done.5, bf16[256,256]{1,0:T(8,128)(2,1)} %collective-permute-done.13, bf16[256,256]{1,0:T(8,128)(2,1)} %collective-permute-done.12, f32[256,256]{1,0:T(8,128)S(1)} %get-tuple-element.26, ...), kind=kLoop, calls=%fused_computation.4 | loop fusion | flops 720896 | bytes 1048576 | tf_op jit(solution)/shard_map/reshape | solution.py:266
  73.2 0.7 fusion.1
  73.9 11.0 %collective-permute-done.8 = bf16[64,4096]{1,0:T(8,128)(2,1)S(1)} collective-permute-done((bf16[64,4096]{1,0:T(8,128)(2,1)S(1)}, bf16[64,4096]{1,0:T(8,128)(2,1)S(1)}, u32[]{:S(2)}, u32[]{:S(2)}) %collective-permute-start.8) | collective-permute-done | bytes 524320 | tf_op jit(solution)/shard_map/ppermute | solution.py:191
  84.8 1.0 %add_convert_fusion = bf16[64,4096]{1,0:T(8,128)(2,1)} fusion(bf16[64,4096]{1,0:T(8,128)(2,1)S(1)} %collective-permute-done.8, bf16[64,4096]{1,0:T(8,128)(2,1)S(1)} %collective-permute-done.6, bf16[64,4096]{1,0:T(8,128)(2,1)S(1)} %get-tuple-element.18), kind=kLoop, calls=%fused_computation | loop fusion | flops 1572864 | bytes 2097152 | tf_op jit(solution)/shard_map/convert_element_type | solution.py:265
  (21 shorter events, 0.1 us)
Async XLA Ops:
  0.6 36.4 %copy-start.3 = (s32[16]{0:T(128)S(1)}, s32[16]{0:T(128)}, u32[]{:S(2)}) copy-start(s32[16]{0:T(128)} %len_ref.3) | copy-start | bytes 196
  0.6 23.7 %collective-permute-start.9 = (bf16[64,4096]{1,0:T(8,128)(2,1)}, bf16[64,4096]{1,0:T(8,128)(2,1)S(1)}, u32[]{:S(2)}, u32[]{:S(2)}) collective-permute-start(bf16[64,4096]{1,0:T(8,128)(2,1)} %refs_6_.1), channel_id=1, source_target_pairs={{0,2},{1,3},{2,0},{3,1},{4,6},{5,7},{6,4},{7,5},{8,10},{9,11},{10,... | collective-permute-start | bytes 1572872 | tf_op jit(solution)/shard_map/ppermute | solution.py:191
  3.7 23.3 %collective-permute-start.5 = (bf16[64,4096]{1,0:T(8,128)(2,1)}, bf16[64,4096]{1,0:T(8,128)(2,1)S(1)}, u32[]{:S(2)}, u32[]{:S(2)}) collective-permute-start(bf16[64,4096]{1,0:T(8,128)(2,1)} %refs_6_.1), channel_id=1, source_target_pairs={{0,1},{1,0},{2,3},{3,2},{4,5},{5,4},{6,7},{7,6},{8,9},{9,8},{10,11... | collective-permute-start | bytes 1572872 | tf_op jit(solution)/shard_map/ppermute | solution.py:191
  4.6 12.2 %collective-permute-start = (bf16[256,256]{1,0:T(8,128)(2,1)S(1)}, bf16[256,256]{1,0:T(8,128)(2,1)S(1)}, u32[]{:S(2)}, u32[]{:S(2)}) collective-permute-start(bf16[256,256]{1,0:T(8,128)(2,1)S(1)} %pad_maximum_fusion.refs_0_), channel_id=1, source_target_pairs={{0,4},{4,8},{8,12},{12,16},{16,20},{20,24},{24,28},{1,5},{5,9},{9,... | collective-permute-start | bytes 393224 | tf_op jit(solution)/shard_map/ppermute | solution.py:195
  8.1 10.5 %collective-permute-start.1 = (bf16[256,256]{1,0:T(8,128)(2,1)S(1)}, bf16[256,256]{1,0:T(8,128)(2,1)S(1)}, u32[]{:S(2)}, u32[]{:S(2)}) collective-permute-start(bf16[256,256]{1,0:T(8,128)(2,1)S(1)} %pad_maximum_fusion.refs_0_), channel_id=1, source_target_pairs={{0,8},{4,12},{8,16},{12,20},{16,24},{20,28},{1,9},{5,13},{9,17},{1... | collective-permute-start | bytes 393224 | tf_op jit(solution)/shard_map/ppermute | solution.py:195
  12.6 12.8 %collective-permute-start.2 = (bf16[256,256]{1,0:T(8,128)(2,1)S(1)}, bf16[256,256]{1,0:T(8,128)(2,1)S(1)}, u32[]{:S(2)}, u32[]{:S(2)}) collective-permute-start(bf16[256,256]{1,0:T(8,128)(2,1)S(1)} %pad_maximum_fusion.refs_0_), channel_id=1, source_target_pairs={{0,12},{4,16},{8,20},{12,24},{16,28},{1,13},{5,17},{9,21},{13,25},... | collective-permute-start | bytes 393224 | tf_op jit(solution)/shard_map/ppermute | solution.py:195
  16.8 8.6 %collective-permute-start.3 = (bf16[256,256]{1,0:T(8,128)(2,1)S(1)}, bf16[256,256]{1,0:T(8,128)(2,1)S(1)}, u32[]{:S(2)}, u32[]{:S(2)}) collective-permute-start(bf16[256,256]{1,0:T(8,128)(2,1)S(1)} %pad_maximum_fusion.refs_0_), channel_id=1, source_target_pairs={{0,16},{4,20},{8,24},{12,28},{1,17},{5,21},{9,25},{13,29},{2,18},{... | collective-permute-start | bytes 393224 | tf_op jit(solution)/shard_map/ppermute | solution.py:195
  18.5 8.4 %collective-permute-start.4 = (bf16[256,256]{1,0:T(8,128)(2,1)S(1)}, bf16[256,256]{1,0:T(8,128)(2,1)S(1)}, u32[]{:S(2)}, u32[]{:S(2)}) collective-permute-start(bf16[256,256]{1,0:T(8,128)(2,1)S(1)} %pad_maximum_fusion.refs_0_), channel_id=1, source_target_pairs={{0,20},{4,24},{8,28},{1,21},{5,25},{9,29},{2,22},{6,26},{10,30},{3... | collective-permute-start | bytes 393224 | tf_op jit(solution)/shard_map/ppermute | solution.py:195
  24.3 12.7 %collective-permute-start.10 = (bf16[64,4096]{1,0:T(8,128)(2,1)S(1)}, bf16[64,4096]{1,0:T(8,128)(2,1)S(1)}, u32[]{:S(2)}, u32[]{:S(2)}) collective-permute-start(bf16[64,4096]{1,0:T(8,128)(2,1)S(1)} %collective-permute-done.9.refs_9_), channel_id=1, source_target_pairs={{0,1},{1,0},{2,3},{3,2},{4,5},{5,4},{6,7},{7,6},{8,9},{9,8},{10,11... | collective-permute-start | bytes 1572872 | tf_op jit(solution)/shard_map/ppermute | solution.py:191
  26.9 2.2 %copy-start = (bf16[4,128,4096]{2,1,0:T(8,128)(2,1)S(1)}, bf16[4,128,4096]{2,1,0:T(8,128)(2,1)}, u32[]{:S(2)}) copy-start(bf16[4,128,4096]{2,1,0:T(8,128)(2,1)} %param.9) | copy-start | bytes 12582916
  29.1 1.0 %copy-start.1 = (bf16[64,4096]{1,0:T(8,128)(2,1)S(1)}, bf16[64,4096]{1,0:T(8,128)(2,1)}, u32[]{:S(2)}) copy-start(bf16[64,4096]{1,0:T(8,128)(2,1)} %refs_6_.1) | copy-start | bytes 1572868
  30.2 0.7 copy-start.2
  36.9 12.3 %collective-permute-start.7 = (bf16[64,4096]{1,0:T(8,128)(2,1)S(1)}, bf16[64,4096]{1,0:T(8,128)(2,1)S(1)}, u32[]{:S(2)}, u32[]{:S(2)}) collective-permute-start(bf16[64,4096]{1,0:T(8,128)(2,1)S(1)} %get-tuple-element.20), channel_id=1, source_target_pairs={{0,1},{1,0},{2,3},{3,2},{4,5},{5,4},{6,7},{7,6},{8,9},{9,8},{10,11... | collective-permute-start | bytes 1572872 | tf_op jit(solution)/shard_map/ppermute | solution.py:191
  44.0 26.5 %collective-permute-start.15 = (bf16[256,256]{1,0:T(8,128)(2,1)S(1)}, bf16[256,256]{1,0:T(8,128)(2,1)S(1)}, u32[]{:S(2)}, u32[]{:S(2)}) collective-permute-start(bf16[256,256]{1,0:T(8,128)(2,1)S(1)} %get-tuple-element.31), channel_id=1, source_target_pairs={{20,0},{24,4},{28,8},{21,1},{25,5},{29,9},{22,2},{26,6},{30,10},{2... | collective-permute-start | bytes 393224 | tf_op jit(solution)/shard_map/ppermute | solution.py:195
  45.3 25.2 %collective-permute-start.14 = (bf16[256,256]{1,0:T(8,128)(2,1)S(1)}, bf16[256,256]{1,0:T(8,128)(2,1)S(1)}, u32[]{:S(2)}, u32[]{:S(2)}) collective-permute-start(bf16[256,256]{1,0:T(8,128)(2,1)S(1)} %get-tuple-element.30), channel_id=1, source_target_pairs={{16,0},{20,4},{24,8},{28,12},{17,1},{21,5},{25,9},{29,13},{18,2},{... | collective-permute-start | bytes 393224 | tf_op jit(solution)/shard_map/ppermute | solution.py:195
  46.6 25.4 %collective-permute-start.13 = (bf16[256,256]{1,0:T(8,128)(2,1)S(1)}, bf16[256,256]{1,0:T(8,128)(2,1)}, u32[]{:S(2)}, u32[]{:S(2)}) collective-permute-start(bf16[256,256]{1,0:T(8,128)(2,1)S(1)} %get-tuple-element.29), channel_id=1, source_target_pairs={{12,0},{16,4},{20,8},{24,12},{28,16},{13,1},{17,5},{21,9},{25,13},... | collective-permute-start | bytes 393224 | tf_op jit(solution)/shard_map/ppermute | solution.py:195
  47.9 24.1 %collective-permute-start.12 = (bf16[256,256]{1,0:T(8,128)(2,1)S(1)}, bf16[256,256]{1,0:T(8,128)(2,1)}, u32[]{:S(2)}, u32[]{:S(2)}) collective-permute-start(bf16[256,256]{1,0:T(8,128)(2,1)S(1)} %get-tuple-element.28), channel_id=1, source_target_pairs={{8,0},{12,4},{16,8},{20,12},{24,16},{28,20},{9,1},{13,5},{17,9},{2... | collective-permute-start | bytes 393224 | tf_op jit(solution)/shard_map/ppermute | solution.py:195
  49.2 22.8 %collective-permute-start.11 = (bf16[256,256]{1,0:T(8,128)(2,1)S(1)}, bf16[256,256]{1,0:T(8,128)(2,1)}, u32[]{:S(2)}, u32[]{:S(2)}) collective-permute-start(bf16[256,256]{1,0:T(8,128)(2,1)S(1)} %get-tuple-element.27), channel_id=1, source_target_pairs={{4,0},{8,4},{12,8},{16,12},{20,16},{24,20},{28,24},{5,1},{9,5},{13... | collective-permute-start | bytes 393224 | tf_op jit(solution)/shard_map/ppermute | solution.py:195
  70.5 0.7 copy-start.4
  70.5 3.4 %collective-permute-start.6 = (bf16[64,4096]{1,0:T(8,128)(2,1)S(1)}, bf16[64,4096]{1,0:T(8,128)(2,1)S(1)}, u32[]{:S(2)}, u32[]{:S(2)}) collective-permute-start(bf16[64,4096]{1,0:T(8,128)(2,1)S(1)} %get-tuple-element.19), channel_id=1, source_target_pairs={{0,1},{1,0},{2,3},{3,2},{4,5},{5,4},{6,7},{7,6},{8,9},{9,8},{10,11... | collective-permute-start | bytes 1572872 | tf_op jit(solution)/shard_map/ppermute | solution.py:191
  70.5 0.7 copy-start.5
  70.5 14.3 %collective-permute-start.8 = (bf16[64,4096]{1,0:T(8,128)(2,1)S(1)}, bf16[64,4096]{1,0:T(8,128)(2,1)S(1)}, u32[]{:S(2)}, u32[]{:S(2)}) collective-permute-start(bf16[64,4096]{1,0:T(8,128)(2,1)S(1)} %add_convert_fusion.1), channel_id=1, source_target_pairs={{0,2},{1,3},{2,0},{3,1},{4,6},{5,7},{6,4},{7,5},{8,10},{9,11},{10,... | collective-permute-start | bytes 1572872 | tf_op jit(solution)/shard_map/ppermute | solution.py:191

commit v2 on v1

v2 whole, which is shorter than its diff:
```python
import functools

import jax
import jax.numpy as jnp
from jax import lax
from jax.experimental import pallas as pl
from jax.experimental.pallas import tpu as pltpu
from jax.sharding import PartitionSpec as P

NEG_FILL = -1e30
LOG2E = 1.4426950408889634
CTX = ("outer", "inner")
F32 = jnp.float32
BF16 = jnp.bfloat16


def dot_nt(a, b):
    return lax.dot_general(a, b, (((1,), (1,)), ((), ())), preferred_element_type=F32)


def dot_nn(a, b):
    return jnp.dot(a, b, preferred_element_type=F32)


def layout_of(len_ref, me, tok):
    offset = me * tok
    q_pos = offset + lax.broadcasted_iota(jnp.int32, (1, tok), 1)
    begin = jnp.zeros((1, tok), jnp.int32)
    first = jnp.int32(0)
    end = jnp.int32(0)
    for j in range(len_ref.shape[0]):
        end = end + len_ref[j]
        begin = jnp.where(q_pos >= end, end, begin)
        first = jnp.where(offset >= end, end, first)
    n_blocks = me - first // tok + 1
    return q_pos, begin, n_blocks


def bias_of(q_pos, begin, k_start, tok):
    k_pos = k_start + lax.broadcasted_iota(jnp.int32, (tok, tok), 0)
    return jnp.where((k_pos >= begin) & (k_pos <= q_pos), 0.0, NEG_FILL).astype(F32)


def stage(kvs, kv_refs, n_blocks):
    for d, ref in enumerate(kv_refs):

        @pl.when(d < n_blocks)
        def _():
            kvs[d] = ref[...]


def d_attn_kernel(own_hbm, pair_hbm, w_hbm, out_ref, w_ref, rows, total, sems):
    core = lax.axis_index("tensor") & 1
    quarter = own_hbm.shape[0]
    width = w_ref.shape[1]
    steps = sems.shape[0] - 2
    step = width // steps
    copies = [
        pltpu.make_async_copy(own_hbm, rows.at[pl.ds(pl.multiple_of(core * quarter, quarter), quarter), :], sems.at[0]),
        pltpu.make_async_copy(
            pair_hbm, rows.at[pl.ds(pl.multiple_of((1 - core) * quarter, quarter), quarter), :], sems.at[1]
        ),
    ]
    for i in range(steps):
        cols = slice(i * step, (i + 1) * step)
        copies.append(pltpu.make_async_copy(w_hbm.at[:, cols], w_ref.at[:, cols], sems.at[2 + i]))
    for copy in copies:
        copy.start()
    copies[0].wait()
    copies[1].wait()
    for i in range(steps):
        cols = slice(i * step, (i + 1) * step)
        copies[2 + i].wait()
        part = dot_nt(rows[:, cols], w_ref[:, cols])
        total[...] = part if i == 0 else total[...] + part
    out_ref[...] = total[...].astype(BF16)


def by_head(ref, out, tok, hd):
    for h in range(ref.shape[1] // hd):
        out[h * tok : (h + 1) * tok, :] = ref[:, h * hd : (h + 1) * hd]


def forward_kernel(lo, n_kv, heads, scale, len_ref, q_ref, *refs):
    kv_refs = refs[:n_kv]
    refs = refs[n_kv:]
    if lo == 0:
        top, denom, acc, kvs, qs = refs
    else:
        top_in, denom_in, acc_in, attn_ref, lse_ref, kvs, qs, top, denom, acc = refs
    tok = q_ref.shape[0]
    hd = q_ref.shape[1] // heads
    me = lax.axis_index(CTX)
    q_pos, begin, n_blocks = layout_of(len_ref, me, tok)
    n_here = jnp.clip(n_blocks - lo, 0, n_kv)
    stage(kvs, kv_refs, n_here)
    by_head(q_ref, qs, tok, hd)
    if lo == 0:
        top[...] = jnp.full(top.shape, NEG_FILL, F32)
        denom[...] = jnp.zeros(denom.shape, F32)
        acc[...] = jnp.zeros(acc.shape, F32)
    else:
        top[...] = top_in[...]
        denom[...] = denom_in[...]
        acc[...] = acc_in[...]

    def block(d, carry):
        k = kvs[d, :, :hd]
        v_t = kvs[d, :, hd:].T
        bias = bias_of(q_pos, begin, (me - lo - d) * tok, tok)
        s = dot_nt(k, qs[...]) * (scale * LOG2E) + jnp.concatenate([bias] * heads, axis=1)
        old = top[...]
        new = jnp.maximum(old, jnp.max(s, axis=0, keepdims=True))
        p = jnp.exp2(s - new)
        shrink = jnp.exp2(old - new)
        top[...] = new
        denom[...] = denom[...] * shrink + jnp.sum(p, axis=0, keepdims=True)
        acc[...] = acc[...] * shrink + dot_nn(v_t, p.astype(BF16))
        return carry

    lax.fori_loop(0, n_here, block, 0)
    if lo == 0:
        return
    lse_ref[...] = top[...] + jnp.log(denom[...]) * LOG2E
    for h in range(heads):
        cols = slice(h * tok, (h + 1) * tok)
        attn_ref[:, h * hd : (h + 1) * hd] = (acc[:, cols] / denom[:, cols]).T.astype(BF16)


def middle_kernel(heads, attn_ref, near_ref, cross_ref, diag_ref, w_ref, *refs):
    send_ref, keep_ref, g_ref, delta_ref, rows, others = refs
    t = lax.axis_index("tensor")
    chip, core = t >> 1, t & 1
    tok = attn_ref.shape[0]
    hd = attn_ref.shape[1] // heads
    quarter, half = tok // 4, tok // 2
    for i, mask in enumerate((3, 1, 2, 0)):
        rows[i * quarter : (i + 1) * quarter, :] = attn_ref[pl.ds(pl.multiple_of((t ^ mask) * quarter, quarter), quarter), :]
    width = w_ref.shape[1]
    step = 512
    for n in range(width // step):
        cols = slice(n * step, (n + 1) * step)
        mixed = dot_nn(rows[...], w_ref[:, cols]).astype(BF16)
        send_ref[:, cols] = mixed[:half, :]
        keep_ref[:, cols] = mixed[half:, :]
    others[pl.ds(pl.multiple_of(core * quarter, quarter), quarter), :] = cross_ref[...]
    others[pl.ds(pl.multiple_of((1 - core) * quarter, quarter), quarter), :] = diag_ref[...]
    g_ref[pl.ds(pl.multiple_of(chip * half, half), half), :] = near_ref[...]
    g_ref[pl.ds(pl.multiple_of((1 - chip) * half, half), half), :] = dot_nt(others[...], w_ref[...]).astype(BF16)
    for h in range(heads):
        part = slice(h * hd, (h + 1) * hd)
        prod = g_ref[:, part].astype(F32) * attn_ref[:, part].astype(F32)
        delta_ref[:, h * tok : (h + 1) * tok] = jnp.sum(prod.T, axis=0, keepdims=True)


def backward_kernel(lo, n_kv, heads, scale, len_ref, q_ref, *refs):
    kv_refs = refs[:n_kv]
    refs = refs[n_kv:]
    if lo == 0:
        g_ref, lse_ref, delta_ref, dq_in = refs[:4]
        dq_ref = refs[4]
        refs = refs[5:]
    else:
        g_ref, lse_ref, delta_ref = refs[:3]
        dq_out = refs[3]
        refs = refs[4:]
    out_refs = refs[:n_kv]
    kvs, terms, qs, gs = refs[n_kv : n_kv + 4]
    dq_t = refs[n_kv + 4] if lo == 0 else dq_out
    tok = q_ref.shape[0]
    hd = q_ref.shape[1] // heads
    me = lax.axis_index(CTX)
    q_pos, begin, n_blocks = layout_of(len_ref, me, tok)
    n_here = jnp.clip(n_blocks - lo, 0, n_kv)
    stage(kvs, kv_refs, n_here)
    by_head(q_ref, qs, tok, hd)
    by_head(g_ref, gs, tok, hd)
    dq_t[...] = dq_in[...] if lo == 0 else jnp.zeros(dq_t.shape, F32)

    def block(d, carry):
        k = kvs[d, :, :hd]
        bias = bias_of(q_pos, begin, (me - lo - d) * tok, tok)
        s = dot_nt(k, qs[...]) * (scale * LOG2E) + jnp.concatenate([bias] * heads, axis=1)
        p = jnp.exp2(s - lse_ref[...])
        dp = dot_nt(kvs[d, :, hd:], gs[...])
        ds = (p * (dp - delta_ref[...])).astype(BF16)
        terms[d, :, :hd] = (dot_nn(ds, qs[...]) * scale).astype(terms.dtype)
        terms[d, :, hd:] = dot_nn(p.astype(BF16), gs[...]).astype(terms.dtype)
        dq_t[...] = dq_t[...] + dot_nn(k.T, ds)
        return carry

    lax.fori_loop(0, n_here, block, 0)
    for d in range(n_kv):

        @pl.when(d < n_here)
        def _():
            out_refs[d][...] = terms[d].astype(out_refs[d].dtype)

        @pl.when(d >= n_here)
        def _():
            out_refs[d][...] = jnp.zeros(out_refs[d].shape, out_refs[d].dtype)

    if lo == 0:
        for h in range(heads):
            dq_ref[:, h * hd : (h + 1) * hd] = (dq_t[:, h * tok : (h + 1) * tok] * scale).T.astype(BF16)


def finish_kernel(*refs):
    dk_ref, dv_ref = refs[-2:]
    total = refs[0][...]
    for ref in refs[1:-2]:
        total = total + ref[...].astype(F32)
    hd = dk_ref.shape[1]
    dk_ref[...] = total[:, :hd].astype(BF16)
    dv_ref[...] = total[:, hd:].astype(BF16)


def pair_sum_kernel(keep_ref, pair_ref, out_ref):
    n = out_ref.shape[0]
    out_ref[...] = (keep_ref[:n, :].astype(F32) + pair_ref[:n, :].astype(F32)).astype(BF16)


def mixed_sum_kernel(keep_ref, pair_ref, cross_ref, out_ref):
    n = out_ref.shape[0]
    total = keep_ref[n:, :].astype(F32) + pair_ref[n:, :].astype(F32) + cross_ref[...].astype(F32)
    out_ref[...] = total.astype(BF16)


def call(kernel, name, out_shape, args, scratch=(), smem=0, hbm=0, us=1.0):
    vmem = pl.BlockSpec(memory_space=pltpu.VMEM)
    return pl.pallas_call(
        kernel,
        out_shape=out_shape,
        in_specs=[pl.BlockSpec(memory_space=pltpu.SMEM)] * smem
        + [pl.BlockSpec(memory_space=pl.ANY)] * hbm
        + [vmem] * (len(args) - smem - hbm),
        out_specs=jax.tree.map(lambda _: vmem, out_shape),
        scratch_shapes=list(scratch),
        compiler_params=pltpu.CompilerParams(vmem_limit_bytes=24 * 2**20),
        cost_estimate=pl.CostEstimate(flops=int(us * 1e9), bytes_accessed=int(us * 3e6), transcendentals=0),
        name=name,
    )(*args)


def local(queries, keys, values, w_out, d_out, lengths):
    tok, heads, hd = queries.shape
    width = w_out.shape[2]
    ctx = lax.axis_size(CTX)
    longest = tok * ctx * 5 // 8
    reach = min(ctx - 1, -(-(longest - 1) // tok))
    n_kv = reach + 1
    split = (n_kv + 1) // 2
    scale = hd ** (-0.5)
    quarter = tok // 4
    n_tensor = lax.axis_size("tensor")
    shape = jax.ShapeDtypeStruct

    def swap(x, mask):
        return lax.ppermute(x, "tensor", [(i, i ^ mask) for i in range(n_tensor)])

    def shift(x, d):
        pairs = [(i, i + d) for i in range(ctx - d)] if d > 0 else [(i - d, i) for i in range(ctx + d)]
        return lax.ppermute(x, CTX, pairs)

    q = queries.reshape(tok, heads * hd)
    kv = jnp.concatenate([keys.reshape(tok, hd), values.reshape(tok, hd)], axis=1)
    w = w_out.reshape(heads * hd, width)
    pair = swap(d_out, 1)
    cross = swap(d_out, 2)
    kv, pair = lax.optimization_barrier((kv, pair))
    kvs = [kv] + [shift(kv, d) for d in range(1, n_kv)]
    half_rows = pltpu.VMEM((tok // 2, width), BF16)
    d_near, w = call(
        d_attn_kernel,
        "d_attn_near",
        (shape((tok // 2, heads * hd), BF16), shape((heads * hd, width), BF16)),
        (d_out, pair, w),
        scratch=(half_rows, pltpu.VMEM((tok // 2, heads * hd), F32), pltpu.SemaphoreType.DMA((10,))),
        hbm=3,
        us=2.0,
    )
    row = shape((1, heads * tok), F32)
    state = (row, row, shape((hd, heads * tok), F32))
    all_rows = pltpu.VMEM((heads * tok, hd), BF16)
    begun = call(
        functools.partial(forward_kernel, 0, split, heads, scale),
        "forward_near",
        state,
        (lengths, q, *kvs[:split]),
        scratch=(pltpu.VMEM((split, tok, 2 * hd), BF16), all_rows),
        smem=1,
        us=4.0,
    )
    attn, lse = call(
        functools.partial(forward_kernel, split, n_kv - split, heads, scale),
        "forward_far",
        (shape((tok, heads * hd), BF16), row),
        (lengths, q, *kvs[split:], *begun),
        scratch=(pltpu.VMEM((n_kv - split, tok, 2 * hd), BF16), all_rows)
        + tuple(pltpu.VMEM(x.shape, F32) for x in state),
        smem=1,
        us=4.0,
    )
    cross, *rest = lax.optimization_barrier((cross, *kvs[1:], d_near))
    d_near = rest[-1]
    diag = swap(cross, 1)
    send, keep, g, delta = call(
        functools.partial(middle_kernel, heads),
        "middle",
        (shape((tok // 2, width), BF16),) * 2 + (shape((tok, heads * hd), BF16), row),
        (attn, d_near, cross, diag, w),
        scratch=(pltpu.VMEM((tok, heads * hd), BF16), half_rows),
        us=3.0,
    )
    from_pair = swap(send, 1)

    def backward(lo, hi, extra):
        n = hi - lo
        dq_shape = shape((tok, heads * hd), BF16) if lo == 0 else state[2]
        outs = tuple(shape((tok, 2 * hd), F32 if lo + i == 0 else BF16) for i in range(n))
        scratch = [pltpu.VMEM((n, tok, 2 * hd), BF16), pltpu.VMEM((n, tok, 2 * hd), F32 if lo == 0 else BF16)]
        scratch += [all_rows, all_rows]
        if lo == 0:
            scratch.append(pltpu.VMEM(state[2].shape, F32))
        dq, *terms = call(
            functools.partial(backward_kernel, lo, n, heads, scale),
            "backward_near" if lo == 0 else "backward_far",
            (dq_shape,) + outs,
            (lengths, q, *kvs[lo:hi], g, lse, delta) + extra,
            scratch=scratch,
            smem=1,
            us=4.0,
        )
        return dq, terms

    dq_t, far_terms = backward(split, n_kv, ())
    to_cross = call(pair_sum_kernel, "pair_sum", shape((quarter, width), BF16), (keep, from_pair), us=0.5)
    from_cross = swap(to_cross, 2)
    far_back = [shift(x, -(split + i)) for i, x in enumerate(far_terms)]
    dq_t, to_cross = lax.optimization_barrier((dq_t, to_cross))
    dq, near_terms = backward(0, split, (dq_t,))
    near_back = [shift(x, -i) for i, x in enumerate(near_terms) if i > 0]
    mixed = call(mixed_sum_kernel, "mixed_sum", shape((quarter, width), BF16), (keep, from_pair, from_cross), us=0.5)
    own, mixed = lax.optimization_barrier((near_terms[0], mixed))
    dk, dv = call(
        finish_kernel,
        "finish",
        (shape((tok, hd), BF16),) * 2,
        (own, *far_back, *near_back),
        us=0.5,
    )
    return (mixed, dq.reshape(tok, heads, hd), dk.reshape(tok, 1, hd), dv.reshape(tok, 1, hd))


def solution(mesh):
    return jax.shard_map(
        local,
        mesh=mesh,
        in_specs=(
            P(("outer", "inner"), "tensor", None),
            P(("outer", "inner"), "tensor", None),
            P(("outer", "inner"), "tensor", None),
            P("tensor", None, None),
            P(("outer", "inner", "tensor"), None),
            P(),
        ),
        out_specs=(
            P(("outer", "inner", "tensor"), None),
            P(("outer", "inner"), "tensor", None),
            P(("outer", "inner"), "tensor", None),
            P(("outer", "inner"), "tensor", None),
        ),
        check_vma=False,
    )
```

time: 84.7 us -> 67.4 us (0.80)
  the two profiles are of different devices: /device:TPU:0 before, /device:TPU:2 now
where the time goes in v2:
time: 67.4 us; the launch traced here: 66.9 us
  starting transfers between devices  25.7 us (38%)
  Pallas kernels  19.9 us (30%)
  waiting for transfers between devices  12.9 us (19%)
  local copies, waits for them, and re-layouts  6.64 us (10%)
  other arithmetic  0.89 us (1%)
  between operations  0.84 us (1%)
    ppermute x10, starting transfers between devices, shift(): return lax.ppermute(x, CTX, pairs)  22.9 us
    pallas_call x9, Pallas kernels, call(): pl.pallas_call(kernel, out_shape=out_shape, in_specs=[pl.BlockSpec(memory...  19.9 us
    ppermute x10, waiting for transfers between devices, shift(): return lax.ppermute(x, CTX, pairs)  9.58 us
    unnamed x11, local copies, waits for them, and re-layouts  5.87 us
    ppermute x5, waiting for transfers between devices, swap(): return lax.ppermute(x, 'tensor', [(i, i ^ mask) for i in range(n_tensor)])  3.32 us
    ppermute x5, starting transfers between devices, swap(): return lax.ppermute(x, 'tensor', [(i, i ^ mask) for i in range(n_tensor)])  2.82 us
  transfers between devices with their start and end apart: 15, of which 5 were waited for; matrix products, arithmetic and copies ran while one was open for 4% of the time, Pallas kernels for 23%

profile of v2, /device:TPU:2, one launch (start us, length us, event | category | flops | bytes accessed | tf_op | source)
XLA Modules:
  0.0 66.9 jit_solution(4185954150411071962)
XLA Ops:
  0.7 1.6 %collective-permute-start.6 = (bf16[64,4096]{1,0:T(8,128)(2,1)}, bf16[64,4096]{1,0:T(8,128)(2,1)S(1)}, u32[]{:S(2)}, u32[]{:S(2)}) collective-permute-start(bf16[64,4096]{1,0:T(8,128)(2,1)} %own_hbm.1), channel_id=1, source_target_pairs={{0,2},{1,3},{2,0},{3,1},{4,6},{5,7},{6,4},{7,5},{8,10},{9,11},{10,... | collective-permute-start | bytes 1572872 | tf_op jit(solution)/shard_map/ppermute | solution.py:259
  2.3 1.0 %copy.12 = bf16[32,8,4,128]{3,1,2,0:T(8,128)(2,1)S(1)} copy(bf16[32,8,4,128]{3,2,1,0:T(4,128)(2,1)} %bitcast.14) | data formatting | bytes 524288
  3.3 0.9 %pad_maximum_fusion.refs_0_ = bf16[256,256]{1,0:T(8,128)(2,1)S(1)} fusion(bf16[256,128]{1,0:T(8,128)(2,1)} %bitcast.15, bf16[256,128]{1,0:T(8,128)(2,1)} %bitcast.16), kind=kLoop, calls=%fused_computation.1 | loop fusion | flops 262144 | bytes 262144 | tf_op jit(solution)/shard_map/concatenate | solution.py:266
  4.2 0.7 collective-permute-start.5
  4.9 1.3 %collective-permute-start.4 = (bf16[256,256]{1,0:T(8,128)(2,1)S(1)}, bf16[256,256]{1,0:T(8,128)(2,1)S(1)}, u32[]{:S(2)}, u32[]{:S(2)}) collective-permute-start(bf16[256,256]{1,0:T(8,128)(2,1)S(1)} %pad_maximum_fusion.refs_0_), channel_id=1, source_target_pairs={{0,16},{4,20},{8,24},{12,28},{1,17},{5,21},{9,25},{13,29},{2,18},{... | collective-permute-start | bytes 393224 | tf_op jit(solution)/shard_map/ppermute | solution.py:263
  6.2 6.1 %collective-permute-start.3 = (bf16[256,256]{1,0:T(8,128)(2,1)S(1)}, bf16[256,256]{1,0:T(8,128)(2,1)S(1)}, u32[]{:S(2)}, u32[]{:S(2)}) collective-permute-start(bf16[256,256]{1,0:T(8,128)(2,1)S(1)} %pad_maximum_fusion.refs_0_), channel_id=1, source_target_pairs={{0,12},{4,16},{8,20},{12,24},{16,28},{1,13},{5,17},{9,21},{13,25},... | collective-permute-start | bytes 393224 | tf_op jit(solution)/shard_map/ppermute | solution.py:263
  12.3 1.9 %collective-permute-start.2 = (bf16[256,256]{1,0:T(8,128)(2,1)S(1)}, bf16[256,256]{1,0:T(8,128)(2,1)S(1)}, u32[]{:S(2)}, u32[]{:S(2)}) collective-permute-start(bf16[256,256]{1,0:T(8,128)(2,1)S(1)} %pad_maximum_fusion.refs_0_), channel_id=1, source_target_pairs={{0,8},{4,12},{8,16},{12,20},{16,24},{20,28},{1,9},{5,13},{9,17},{1... | collective-permute-start | bytes 393224 | tf_op jit(solution)/shard_map/ppermute | solution.py:263
  14.2 1.0 %collective-permute-done.6.cross_ref = bf16[64,4096]{1,0:T(8,128)(2,1)S(1)} collective-permute-done((bf16[64,4096]{1,0:T(8,128)(2,1)}, bf16[64,4096]{1,0:T(8,128)(2,1)S(1)}, u32[]{:S(2)}, u32[]{:S(2)}) %collective-permute-start.6) | collective-permute-done | bytes 524320 | tf_op jit(solution)/shard_map/ppermute | solution.py:259
  15.3 3.5 %collective-permute-start.1 = (bf16[256,256]{1,0:T(8,128)(2,1)S(1)}, bf16[256,256]{1,0:T(8,128)(2,1)S(1)}, u32[]{:S(2)}, u32[]{:S(2)}) collective-permute-start(bf16[256,256]{1,0:T(8,128)(2,1)S(1)} %pad_maximum_fusion.refs_0_), channel_id=1, source_target_pairs={{0,4},{4,8},{8,12},{12,16},{16,20},{20,24},{24,28},{1,5},{5,9},{9,... | collective-permute-start | bytes 393224 | tf_op jit(solution)/shard_map/ppermute | solution.py:263
  18.8 2.2 %copy-done = bf16[4,128,4096]{2,1,0:T(8,128)(2,1)S(1)} copy-done((bf16[4,128,4096]{2,1,0:T(8,128)(2,1)S(1)}, bf16[4,128,4096]{2,1,0:T(8,128)(2,1)}, u32[]{:S(2)}) %copy-start) | copy-done | bytes 4194328
  20.9 1.0 %copy-done.1 = bf16[64,4096]{1,0:T(8,128)(2,1)S(1)} copy-done((bf16[64,4096]{1,0:T(8,128)(2,1)S(1)}, bf16[64,4096]{1,0:T(8,128)(2,1)}, u32[]{:S(2)}) %copy-start.1) | copy-done | bytes 524312
  22.0 2.4 %d_attn_near.1 = (bf16[128,512]{1,0:T(8,128)(2,1)S(1)}, bf16[512,4096]{1,0:T(8,128)(2,1)S(1)}) custom-call(bf16[64,4096]{1,0:T(8,128)(2,1)S(1)} %copy-done.1, bf16[64,4096]{1,0:T(8,128)(2,1)S(1)} %collective-permute-done.pair_hbm, bf16[512,4096]{1,0:T(8,128)(2,1)S(1)} %bitcast.13), custom_call_target="tpu_custom_call" | custom-call | flops 2000000000 | bytes 6000000 | tf_op jit(solution)/shard_map/d_attn_near/pallas_call | solution.py:231
  24.5 1.8 %collective-permute-done.2.refs_2_ = bf16[256,256]{1,0:T(8,128)(2,1)S(1)} collective-permute-done((bf16[256,256]{1,0:T(8,128)(2,1)S(1)}, bf16[256,256]{1,0:T(8,128)(2,1)S(1)}, u32[]{:S(2)}, u32[]{:S(2)}) %collective-permute-start.2) | collective-permute-done | bytes 131104 | tf_op jit(solution)/shard_map/ppermute | solution.py:263
  26.3 2.7 %forward_near.1 = (f32[1,1024]{1,0:T(1,128)S(1)}, f32[1,1024]{1,0:T(1,128)S(1)}, f32[128,1024]{1,0:T(8,128)S(1)}) custom-call(s32[16]{0:T(128)S(1)} %copy-done.2, bf16[256,512]{1,0:T(8,128)(2,1)S(1)} %bitcast.9, bf16[256,256]{1,0:T(8,128)(2,1)S(1)} %pad_maximum_fusion.refs_0_, bf16[256,256]{1,0:T(8,128)(2,1)S(1)} %collective-permute-done.1.refs_1_, ...), custom_call_target="tpu_custom_call" | custom-call | flops 4000000000 | bytes 12000000 | tf_op jit(solution)/shard_map/forward_near/pallas_call | solution.py:231
  29.0 2.2 %forward_far.1 = (bf16[256,512]{1,0:T(8,128)(2,1)S(1)}, f32[1,1024]{1,0:T(1,128)S(1)}) custom-call(s32[16]{0:T(128)S(1)} %copy-done.2, bf16[256,512]{1,0:T(8,128)(2,1)S(1)} %bitcast.10, bf16[256,256]{1,0:T(8,128)(2,1)S(1)} %collective-permute-done.3.refs_0_, bf16[256,256]{1,0:T(8,128)(2,1)S(1)} %collective-permute-done.4.refs_1_, ...), custom_call_target="tpu_custom_call" | custom-call | flops 4000000000 | bytes 12000000 | tf_op jit(solution)/shard_map/forward_far/pallas_call | solution.py:231
  31.2 2.9 %middle.1 = (bf16[128,4096]{1,0:T(8,128)(2,1)S(1)}, bf16[128,4096]{1,0:T(8,128)(2,1)S(1)}, bf16[256,512]{1,0:T(8,128)(2,1)S(1)}, f32[1,1024]{1,0:T(1,128)S(1)}) custom-call(bf16[256,512]{1,0:T(8,128)(2,1)S(1)} %get-tuple-element.36.attn_ref, bf16[128,512]{1,0:T(8,128)(2,1)S(1)} %get-tuple-element.39.near_ref, ...), custom_call_target="tpu_custom_call" | custom-call | flops 3000000000 | bytes 9000000 | tf_op jit(solution)/shard_map/middle/pallas_call | solution.py:231
  34.7 2.3 %collective-permute-done.8.pair_ref = bf16[128,4096]{1,0:T(8,128)(2,1)S(1)} collective-permute-done((bf16[128,4096]{1,0:T(8,128)(2,1)S(1)}, bf16[128,4096]{1,0:T(8,128)(2,1)S(1)}, u32[]{:S(2)}, u32[]{:S(2)}) %collective-permute-start.8) | collective-permute-done | bytes 1048608 | tf_op jit(solution)/shard_map/ppermute | solution.py:259
  37.1 0.6 collective-permute-start.9
  37.7 3.0 %backward_far.1 = (f32[128,1024]{1,0:T(8,128)S(1)}, bf16[256,256]{1,0:T(8,128)(2,1)}, bf16[256,256]{1,0:T(8,128)(2,1)S(1)}, bf16[256,256]{1,0:T(8,128)(2,1)S(1)}) custom-call(s32[16]{0:T(128)S(1)} %copy-done.2, bf16[256,512]{1,0:T(8,128)(2,1)S(1)} %bitcast.11, bf16[256,256]{1,0:T(8,128)(2,1)S(1)} %collective-permute-done.3.refs_0_, ...), custom_call_target="tpu_custom_call" | custom-call | flops 4000000000 | bytes 12000000 | tf_op jit(solution)/shard_map/backward_far/pallas_call | solution.py:231
  40.7 1.9 %collective-permute-start.10 = (bf16[256,256]{1,0:T(8,128)(2,1)}, bf16[256,256]{1,0:T(8,128)(2,1)S(1)}, u32[]{:S(2)}, u32[]{:S(2)}) collective-permute-start(bf16[256,256]{1,0:T(8,128)(2,1)} %get-tuple-element.53), channel_id=1, source_target_pairs={{12,0},{16,4},{20,8},{24,12},{28,16},{13,1},{17,5},{21,9},{25,13},... | collective-permute-start | bytes 393224 | tf_op jit(solution)/shard_map/ppermute | solution.py:263
  42.6 1.3 %collective-permute-start.11 = (bf16[256,256]{1,0:T(8,128)(2,1)S(1)}, bf16[256,256]{1,0:T(8,128)(2,1)S(1)}, u32[]{:S(2)}, u32[]{:S(2)}) collective-permute-start(bf16[256,256]{1,0:T(8,128)(2,1)S(1)} %get-tuple-element.54), channel_id=1, source_target_pairs={{16,0},{20,4},{24,8},{28,12},{17,1},{21,5},{25,9},{29,13},{18,2},{... | collective-permute-start | bytes 393224 | tf_op jit(solution)/shard_map/ppermute | solution.py:263
  43.9 0.7 collective-permute-start.12
  44.6 3.9 %backward_near.1 = (bf16[256,512]{1,0:T(8,128)(2,1)S(1)}, f32[256,256]{1,0:T(8,128)S(1)}, bf16[256,256]{1,0:T(8,128)(2,1)}, bf16[256,256]{1,0:T(8,128)(2,1)}) custom-call(s32[16]{0:T(128)S(1)} %copy-done.2, bf16[256,512]{1,0:T(8,128)(2,1)S(1)} %bitcast.12, bf16[256,256]{1,0:T(8,128)(2,1)S(1)} %pad_maximum_fusion.refs_0_, ...), custom_call_target="tpu_custom_call" | custom-call | flops 4000000000 | bytes 12000000 | tf_op jit(solution)/shard_map/backward_near/pallas_call | solution.py:231
  48.5 0.7 %copy-done.3 = f32[256,256]{1,0:T(8,128)} copy-done((f32[256,256]{1,0:T(8,128)}, f32[256,256]{1,0:T(8,128)S(1)}, u32[]{:S(2)}) %copy-start.3) | copy-done | bytes 262168
  49.2 3.6 %collective-permute-start.13 = (bf16[256,256]{1,0:T(8,128)(2,1)}, bf16[256,256]{1,0:T(8,128)(2,1)}, u32[]{:S(2)}, u32[]{:S(2)}) collective-permute-start(bf16[256,256]{1,0:T(8,128)(2,1)} %get-tuple-element.56), channel_id=1, source_target_pairs={{4,0},{8,4},{12,8},{16,12},{20,16},{24,20},{28,24},{5,1},{9,5},{13... | collective-permute-start | bytes 393224 | tf_op jit(solution)/shard_map/ppermute | solution.py:263
  52.8 1.9 %collective-permute-start.14 = (bf16[256,256]{1,0:T(8,128)(2,1)}, bf16[256,256]{1,0:T(8,128)(2,1)}, u32[]{:S(2)}, u32[]{:S(2)}) collective-permute-start(bf16[256,256]{1,0:T(8,128)(2,1)} %get-tuple-element.57), channel_id=1, source_target_pairs={{8,0},{12,4},{16,8},{20,12},{24,16},{28,20},{9,1},{13,5},{17,9},{2... | collective-permute-start | bytes 393224 | tf_op jit(solution)/shard_map/ppermute | solution.py:263
  54.7 0.8 %reshape.33 = bf16[256,4,128]{2,1,0:T(4,128)(2,1)} reshape(bf16[256,512]{1,0:T(8,128)(2,1)S(1)} %get-tuple-element.51) | data formatting | bytes 524288 | tf_op jit(solution)/shard_map/reshape | solution.py:352
  55.5 1.0 %mixed_sum.1 = bf16[64,4096]{1,0:T(8,128)(2,1)} custom-call(bf16[128,4096]{1,0:T(8,128)(2,1)S(1)} %get-tuple-element.46.keep_ref, bf16[128,4096]{1,0:T(8,128)(2,1)S(1)} %collective-permute-done.8.pair_ref, bf16[64,4096]{1,0:T(8,128)(2,1)S(1)} %collective-permute-done.9.cross_ref), custom_call_target="tpu_custom_call" | custom-call | flops 500000000 | bytes 1500000 | tf_op jit(solution)/shard_map/mixed_sum/pallas_call | solution.py:231
  56.5 1.0 %collective-permute-done.13.refs_4_ = bf16[256,256]{1,0:T(8,128)(2,1)} collective-permute-done((bf16[256,256]{1,0:T(8,128)(2,1)}, bf16[256,256]{1,0:T(8,128)(2,1)}, u32[]{:S(2)}, u32[]{:S(2)}) %collective-permute-start.13) | collective-permute-done | bytes 131104 | tf_op jit(solution)/shard_map/ppermute | solution.py:263
  57.5 6.8 %collective-permute-done.14.refs_5_ = bf16[256,256]{1,0:T(8,128)(2,1)} collective-permute-done((bf16[256,256]{1,0:T(8,128)(2,1)}, bf16[256,256]{1,0:T(8,128)(2,1)}, u32[]{:S(2)}, u32[]{:S(2)}) %collective-permute-start.14) | collective-permute-done | bytes 131104 | tf_op jit(solution)/shard_map/ppermute | solution.py:263
  64.3 0.9 %copy-done.4 = f32[256,256]{1,0:T(8,128)S(1)} copy-done((f32[256,256]{1,0:T(8,128)S(1)}, f32[256,256]{1,0:T(8,128)}, u32[]{:S(2)}) %copy-start.4) | copy-done | bytes 262168
  65.2 1.7 %finish.1 = (bf16[256,128]{1,0:T(8,128)(2,1)}, bf16[256,128]{1,0:T(8,128)(2,1)}) custom-call(f32[256,256]{1,0:T(8,128)S(1)} %copy-done.4, bf16[256,256]{1,0:T(8,128)(2,1)S(1)} %collective-permute-done.10.refs_1_, bf16[256,256]{1,0:T(8,128)(2,1)S(1)} %collective-permute-done.11.refs_2_, bf16[256,256]{1,0:T(8,128)(2,1)S(1)} %collective-permute-done.12.refs_3_, ...), custom_call_target="tpu_custom_call" | custom-call | flops 500000000 | bytes 1500000 | tf_op jit(solution)/shard_map/finish/pallas_call | solution.py:231
  (20 shorter events, 0.8 us)
Async XLA Ops:
  0.6 25.6 %copy-start.2 = (s32[16]{0:T(128)S(1)}, s32[16]{0:T(128)}, u32[]{:S(2)}) copy-start(s32[16]{0:T(128)} %len_ref.7) | copy-start | bytes 196
  0.6 3.6 %collective-permute-start = (bf16[64,4096]{1,0:T(8,128)(2,1)}, bf16[64,4096]{1,0:T(8,128)(2,1)S(1)}, u32[]{:S(2)}, u32[]{:S(2)}) collective-permute-start(bf16[64,4096]{1,0:T(8,128)(2,1)} %own_hbm.1), channel_id=1, source_target_pairs={{0,1},{1,0},{2,3},{3,2},{4,5},{5,4},{6,7},{7,6},{8,9},{9,8},{10,11... | collective-permute-start | bytes 1572872 | tf_op jit(solution)/shard_map/ppermute | solution.py:259
  0.7 14.5 %collective-permute-start.6 = (bf16[64,4096]{1,0:T(8,128)(2,1)}, bf16[64,4096]{1,0:T(8,128)(2,1)S(1)}, u32[]{:S(2)}, u32[]{:S(2)}) collective-permute-start(bf16[64,4096]{1,0:T(8,128)(2,1)} %own_hbm.1), channel_id=1, source_target_pairs={{0,2},{1,3},{2,0},{3,1},{4,6},{5,7},{6,4},{7,5},{8,10},{9,11},{10,... | collective-permute-start | bytes 1572872 | tf_op jit(solution)/shard_map/ppermute | solution.py:259
  4.2 20.2 %collective-permute-start.5 = (bf16[256,256]{1,0:T(8,128)(2,1)S(1)}, bf16[256,256]{1,0:T(8,128)(2,1)S(1)}, u32[]{:S(2)}, u32[]{:S(2)}) collective-permute-start(bf16[256,256]{1,0:T(8,128)(2,1)S(1)} %pad_maximum_fusion.refs_0_), channel_id=1, source_target_pairs={{0,20},{4,24},{8,28},{1,21},{5,25},{9,29},{2,22},{6,26},{10,30},{3... | collective-permute-start | bytes 393224 | tf_op jit(solution)/shard_map/ppermute | solution.py:263
  4.9 19.6 %collective-permute-start.4 = (bf16[256,256]{1,0:T(8,128)(2,1)S(1)}, bf16[256,256]{1,0:T(8,128)(2,1)S(1)}, u32[]{:S(2)}, u32[]{:S(2)}) collective-permute-start(bf16[256,256]{1,0:T(8,128)(2,1)S(1)} %pad_maximum_fusion.refs_0_), channel_id=1, source_target_pairs={{0,16},{4,20},{8,24},{12,28},{1,17},{5,21},{9,25},{13,29},{2,18},{... | collective-permute-start | bytes 393224 | tf_op jit(solution)/shard_map/ppermute | solution.py:263
  6.2 18.3 %collective-permute-start.3 = (bf16[256,256]{1,0:T(8,128)(2,1)S(1)}, bf16[256,256]{1,0:T(8,128)(2,1)S(1)}, u32[]{:S(2)}, u32[]{:S(2)}) collective-permute-start(bf16[256,256]{1,0:T(8,128)(2,1)S(1)} %pad_maximum_fusion.refs_0_), channel_id=1, source_target_pairs={{0,12},{4,16},{8,20},{12,24},{16,28},{1,13},{5,17},{9,21},{13,25},... | collective-permute-start | bytes 393224 | tf_op jit(solution)/shard_map/ppermute | solution.py:263
  12.3 13.9 %collective-permute-start.2 = (bf16[256,256]{1,0:T(8,128)(2,1)S(1)}, bf16[256,256]{1,0:T(8,128)(2,1)S(1)}, u32[]{:S(2)}, u32[]{:S(2)}) collective-permute-start(bf16[256,256]{1,0:T(8,128)(2,1)S(1)} %pad_maximum_fusion.refs_0_), channel_id=1, source_target_pairs={{0,8},{4,12},{8,16},{12,20},{16,24},{20,28},{1,9},{5,13},{9,17},{1... | collective-permute-start | bytes 393224 | tf_op jit(solution)/shard_map/ppermute | solution.py:263
  15.3 11.0 %collective-permute-start.1 = (bf16[256,256]{1,0:T(8,128)(2,1)S(1)}, bf16[256,256]{1,0:T(8,128)(2,1)S(1)}, u32[]{:S(2)}, u32[]{:S(2)}) collective-permute-start(bf16[256,256]{1,0:T(8,128)(2,1)S(1)} %pad_maximum_fusion.refs_0_), channel_id=1, source_target_pairs={{0,4},{4,8},{8,12},{12,16},{16,20},{20,24},{24,28},{1,5},{5,9},{9,... | collective-permute-start | bytes 393224 | tf_op jit(solution)/shard_map/ppermute | solution.py:263
  18.8 2.2 %copy-start = (bf16[4,128,4096]{2,1,0:T(8,128)(2,1)S(1)}, bf16[4,128,4096]{2,1,0:T(8,128)(2,1)}, u32[]{:S(2)}) copy-start(bf16[4,128,4096]{2,1,0:T(8,128)(2,1)} %param.9) | copy-start | bytes 12582916
  20.9 1.0 %copy-start.1 = (bf16[64,4096]{1,0:T(8,128)(2,1)S(1)}, bf16[64,4096]{1,0:T(8,128)(2,1)}, u32[]{:S(2)}) copy-start(bf16[64,4096]{1,0:T(8,128)(2,1)} %own_hbm.1) | copy-start | bytes 1572868
  26.3 5.0 %collective-permute-start.7 = (bf16[64,4096]{1,0:T(8,128)(2,1)S(1)}, bf16[64,4096]{1,0:T(8,128)(2,1)S(1)}, u32[]{:S(2)}, u32[]{:S(2)}) collective-permute-start(bf16[64,4096]{1,0:T(8,128)(2,1)S(1)} %collective-permute-done.6.cross_ref), channel_id=1, source_target_pairs={{0,1},{1,0},{2,3},{3,2},{4,5},{5,4},{6,7},{7,6},{8,9},{9,8},{10,11... | collective-permute-start | bytes 1572872 | tf_op jit(solution)/shard_map/ppermute | solution.py:259
  34.1 2.9 %collective-permute-start.8 = (bf16[128,4096]{1,0:T(8,128)(2,1)S(1)}, bf16[128,4096]{1,0:T(8,128)(2,1)S(1)}, u32[]{:S(2)}, u32[]{:S(2)}) collective-permute-start(bf16[128,4096]{1,0:T(8,128)(2,1)S(1)} %get-tuple-element.47), channel_id=1, source_target_pairs={{0,1},{1,0},{2,3},{3,2},{4,5},{5,4},{6,7},{7,6},{8,9},{9,8},{10,11... | collective-permute-start | bytes 3145736 | tf_op jit(solution)/shard_map/ppermute | solution.py:259
  37.1 15.7 %collective-permute-start.9 = (bf16[64,4096]{1,0:T(8,128)(2,1)S(1)}, bf16[64,4096]{1,0:T(8,128)(2,1)S(1)}, u32[]{:S(2)}, u32[]{:S(2)}) collective-permute-start(bf16[64,4096]{1,0:T(8,128)(2,1)S(1)} %pair_sum.1), channel_id=1, source_target_pairs={{0,2},{1,3},{2,0},{3,1},{4,6},{5,7},{6,4},{7,5},{8,10},{9,11},{10,... | collective-permute-start | bytes 1572872 | tf_op jit(solution)/shard_map/ppermute | solution.py:259
  40.7 15.8 %collective-permute-start.10 = (bf16[256,256]{1,0:T(8,128)(2,1)}, bf16[256,256]{1,0:T(8,128)(2,1)S(1)}, u32[]{:S(2)}, u32[]{:S(2)}) collective-permute-start(bf16[256,256]{1,0:T(8,128)(2,1)} %get-tuple-element.53), channel_id=1, source_target_pairs={{12,0},{16,4},{20,8},{24,12},{28,16},{13,1},{17,5},{21,9},{25,13},... | collective-permute-start | bytes 393224 | tf_op jit(solution)/shard_map/ppermute | solution.py:263
  42.6 13.9 %collective-permute-start.11 = (bf16[256,256]{1,0:T(8,128)(2,1)S(1)}, bf16[256,256]{1,0:T(8,128)(2,1)S(1)}, u32[]{:S(2)}, u32[]{:S(2)}) collective-permute-start(bf16[256,256]{1,0:T(8,128)(2,1)S(1)} %get-tuple-element.54), channel_id=1, source_target_pairs={{16,0},{20,4},{24,8},{28,12},{17,1},{21,5},{25,9},{29,13},{18,2},{... | collective-permute-start | bytes 393224 | tf_op jit(solution)/shard_map/ppermute | solution.py:263
  43.9 12.6 %collective-permute-start.12 = (bf16[256,256]{1,0:T(8,128)(2,1)S(1)}, bf16[256,256]{1,0:T(8,128)(2,1)S(1)}, u32[]{:S(2)}, u32[]{:S(2)}) collective-permute-start(bf16[256,256]{1,0:T(8,128)(2,1)S(1)} %get-tuple-element.55), channel_id=1, source_target_pairs={{20,0},{24,4},{28,8},{21,1},{25,5},{29,9},{22,2},{26,6},{30,10},{2... | collective-permute-start | bytes 393224 | tf_op jit(solution)/shard_map/ppermute | solution.py:263
  48.5 0.7 %copy-start.3 = (f32[256,256]{1,0:T(8,128)}, f32[256,256]{1,0:T(8,128)S(1)}, u32[]{:S(2)}) copy-start(f32[256,256]{1,0:T(8,128)S(1)} %get-tuple-element.52.refs_0_) | copy-start | bytes 786436
  49.2 8.3 %collective-permute-start.13 = (bf16[256,256]{1,0:T(8,128)(2,1)}, bf16[256,256]{1,0:T(8,128)(2,1)}, u32[]{:S(2)}, u32[]{:S(2)}) collective-permute-start(bf16[256,256]{1,0:T(8,128)(2,1)} %get-tuple-element.56), channel_id=1, source_target_pairs={{4,0},{8,4},{12,8},{16,12},{20,16},{24,20},{28,24},{5,1},{9,5},{13... | collective-permute-start | bytes 393224 | tf_op jit(solution)/shard_map/ppermute | solution.py:263
  52.8 11.5 %collective-permute-start.14 = (bf16[256,256]{1,0:T(8,128)(2,1)}, bf16[256,256]{1,0:T(8,128)(2,1)}, u32[]{:S(2)}, u32[]{:S(2)}) collective-permute-start(bf16[256,256]{1,0:T(8,128)(2,1)} %get-tuple-element.57), channel_id=1, source_target_pairs={{8,0},{12,4},{16,8},{20,12},{24,16},{28,20},{9,1},{13,5},{17,9},{2... | collective-permute-start | bytes 393224 | tf_op jit(solution)/shard_map/ppermute | solution.py:263
  64.3 1.0 %copy-start.4 = (f32[256,256]{1,0:T(8,128)S(1)}, f32[256,256]{1,0:T(8,128)}, u32[]{:S(2)}) copy-start(f32[256,256]{1,0:T(8,128)} %copy-done.3) | copy-start | bytes 786436

commit v3 on v2

v3 whole, which is shorter than its diff:
```python
import functools

import jax
import jax.numpy as jnp
from jax import lax
from jax.experimental import pallas as pl
from jax.experimental.pallas import tpu as pltpu
from jax.sharding import PartitionSpec as P

NEG_FILL = -1e30
LOG2E = 1.4426950408889634
CTX = ("outer", "inner")
F32 = jnp.float32
BF16 = jnp.bfloat16


def dot_nt(a, b):
    return lax.dot_general(a, b, (((1,), (1,)), ((), ())), preferred_element_type=F32)


def dot_nn(a, b):
    return jnp.dot(a, b, preferred_element_type=F32)


def layout_of(len_ref, me, tok):
    offset = me * tok
    q_pos = offset + lax.broadcasted_iota(jnp.int32, (1, tok), 1)
    begin = jnp.zeros((1, tok), jnp.int32)
    first = jnp.int32(0)
    end = jnp.int32(0)
    for j in range(len_ref.shape[0]):
        end = end + len_ref[j]
        begin = jnp.where(q_pos >= end, end, begin)
        first = jnp.where(offset >= end, end, first)
    n_blocks = me - first // tok + 1
    return q_pos, begin, n_blocks


def bias_of(q_pos, begin, k_start, tok):
    k_pos = k_start + lax.broadcasted_iota(jnp.int32, (tok, tok), 0)
    return jnp.where((k_pos >= begin) & (k_pos <= q_pos), 0.0, NEG_FILL).astype(F32)


UNROLL = 8


def each_block(blocks, kv_refs, held, n_blocks, work):
    if len(blocks) <= UNROLL:
        for i, d in enumerate(blocks):

            @pl.when(d < n_blocks)
            def _():
                work(i, d, kv_refs[i])

        return
    for i, d in enumerate(blocks):

        @pl.when(d < n_blocks)
        def _():
            held[i] = kv_refs[i][...]

    def step(i, carry):
        work(i, blocks[0] + i, held.at[i])
        return carry

    lax.fori_loop(0, jnp.clip(n_blocks - blocks[0], 0, len(blocks)), step, 0)


def begin_kernel(len_ref, out_ref):
    tok = out_ref.shape[1]
    _, begin, _ = layout_of(len_ref, lax.axis_index(CTX), tok)
    out_ref[...] = begin


def d_attn_kernel(own_ref, pair_ref, w_ref, out_ref, rows):
    core = lax.axis_index("tensor") & 1
    quarter = own_ref.shape[0]
    rows[pl.ds(pl.multiple_of(core * quarter, quarter), quarter), :] = own_ref[...]
    rows[pl.ds(pl.multiple_of((1 - core) * quarter, quarter), quarter), :] = pair_ref[...]
    out_ref[...] = dot_nt(rows[...], w_ref[...]).astype(BF16)


def forward_kernel(blocks, heads, scale, len_ref, begin_ref, q_ref, *refs):
    n = len(blocks)
    kv_refs = refs[:n]
    if blocks[0] == 0:
        top, denom, acc, held = refs[n:]
    else:
        top_in, denom_in, acc_in, attn_ref, lse_ref, held, top, denom, acc = refs[n:]
    tok, hd = q_ref.shape[0] // heads, q_ref.shape[1]
    me = lax.axis_index(CTX)
    q_pos, _, n_blocks = layout_of(len_ref, me, tok)
    begin = begin_ref[...]
    if blocks[0] == 0:
        top[...] = jnp.full(top.shape, NEG_FILL, F32)
        denom[...] = jnp.zeros(denom.shape, F32)
        acc[...] = jnp.zeros(acc.shape, F32)
    else:
        top[...] = top_in[...]
        denom[...] = denom_in[...]
        acc[...] = acc_in[...]

    def work(i, d, kv):
        v_t = kv[:, hd:].T
        bias = bias_of(q_pos, begin, (me - d) * tok, tok)
        s = dot_nt(kv[:, :hd], q_ref[...]) * (scale * LOG2E) + jnp.concatenate([bias] * heads, axis=1)
        old = top[...]
        new = jnp.maximum(old, jnp.max(s, axis=0, keepdims=True))
        p = jnp.exp2(s - new)
        shrink = jnp.exp2(old - new)
        top[...] = new
        denom[...] = denom[...] * shrink + jnp.sum(p, axis=0, keepdims=True)
        acc[...] = acc[...] * shrink + dot_nn(v_t, p.astype(BF16))

    each_block(blocks, kv_refs, held, n_blocks, work)
    if blocks[0] == 0:
        return
    lse_ref[...] = top[...] + jnp.log(denom[...]) * LOG2E
    for h in range(heads):
        cols = slice(h * tok, (h + 1) * tok)
        attn_ref[:, h * hd : (h + 1) * hd] = (acc[:, cols] / denom[:, cols]).T.astype(BF16)


def middle_kernel(heads, attn_ref, near_ref, cross_ref, diag_ref, w_ref, *refs):
    send_ref, keep_ref, g_ref, delta_ref, rows, others = refs
    t = lax.axis_index("tensor")
    chip, core = t >> 1, t & 1
    tok = attn_ref.shape[0]
    hd = attn_ref.shape[1] // heads
    quarter, half = tok // 4, tok // 2
    for i, mask in enumerate((3, 1, 2, 0)):
        rows[i * quarter : (i + 1) * quarter, :] = attn_ref[pl.ds(pl.multiple_of((t ^ mask) * quarter, quarter), quarter), :]
    width = w_ref.shape[1]
    step = 512
    for n in range(width // step):
        cols = slice(n * step, (n + 1) * step)
        mixed = dot_nn(rows[...], w_ref[:, cols]).astype(BF16)
        send_ref[:, cols] = mixed[:half, :]
        keep_ref[:, cols] = mixed[half:, :]
    others[pl.ds(pl.multiple_of(core * quarter, quarter), quarter), :] = cross_ref[...]
    others[pl.ds(pl.multiple_of((1 - core) * quarter, quarter), quarter), :] = diag_ref[...]
    far = dot_nt(others[...], w_ref[...]).astype(BF16)
    for h in range(heads):
        part = slice(h * hd, (h + 1) * hd)
        g_ref[pl.ds(pl.multiple_of(h * tok + chip * half, half), half), :] = near_ref[:, part]
        g_ref[pl.ds(pl.multiple_of(h * tok + (1 - chip) * half, half), half), :] = far[:, part]
        cols = slice(h * tok, (h + 1) * tok)
        prod = g_ref[cols, :].astype(F32) * attn_ref[:, part].astype(F32)
        delta_ref[:, cols] = jnp.sum(prod.T, axis=0, keepdims=True)


def backward_kernel(blocks, first, last, heads, scale, len_ref, begin_ref, q_ref, *refs):
    n = len(blocks)
    kv_refs = refs[:n]
    g_ref, lse_ref, delta_ref = refs[n : n + 3]
    refs = refs[n + 3 :]
    if not first:
        dq_in, *refs = refs
    if last:
        dq_ref, *refs = refs
    else:
        dq_t, *refs = refs
    out_refs = refs[:n]
    held, terms = refs[n : n + 2]
    if last:
        dq_t = refs[n + 2]
    tok, hd = q_ref.shape[0] // heads, q_ref.shape[1]
    me = lax.axis_index(CTX)
    q_pos, _, n_blocks = layout_of(len_ref, me, tok)
    begin = begin_ref[...]
    dq_t[...] = jnp.zeros(dq_t.shape, F32) if first else dq_in[...]

    def work(i, d, kv):
        k = kv[:, :hd]
        bias = bias_of(q_pos, begin, (me - d) * tok, tok)
        s = dot_nt(k, q_ref[...]) * (scale * LOG2E) + jnp.concatenate([bias] * heads, axis=1)
        p = jnp.exp2(s - lse_ref[...])
        dp = dot_nt(kv[:, hd:], g_ref[...])
        ds = (p * (dp - delta_ref[...])).astype(BF16)
        out = out_refs[i] if n <= UNROLL else terms.at[i]
        out[:, :hd] = (dot_nn(ds, q_ref[...]) * scale).astype(BF16)
        out[:, hd:] = dot_nn(p.astype(BF16), g_ref[...]).astype(BF16)
        dq_t[...] = dq_t[...] + dot_nn(k.T, ds)

    each_block(blocks, kv_refs, held, n_blocks, work)
    for i, d in enumerate(blocks):
        if n > UNROLL:

            @pl.when(d < n_blocks)
            def _():
                out_refs[i][...] = terms[i]

        @pl.when(d >= n_blocks)
        def _():
            out_refs[i][...] = jnp.zeros(out_refs[i].shape, BF16)

    if last:
        for h in range(heads):
            dq_ref[:, h * hd : (h + 1) * hd] = (dq_t[:, h * tok : (h + 1) * tok] * scale).T.astype(BF16)


def finish_kernel(n_kv, *refs):
    sources = refs[:n_kv]
    dk_ref, dv_ref, held, sems = refs[n_kv:]
    copies = [pltpu.make_async_copy(ref, held.at[d], sems.at[d]) for d, ref in enumerate(sources)]
    for copy in copies:
        copy.start()
    for copy in copies:
        copy.wait()
    total = held[0].astype(F32)
    for d in range(1, n_kv):
        total = total + held[d].astype(F32)
    hd = dk_ref.shape[1]
    dk_ref[...] = total[:, :hd].astype(BF16)
    dv_ref[...] = total[:, hd:].astype(BF16)


def pair_sum_kernel(keep_ref, pair_ref, out_ref):
    n = out_ref.shape[0]
    out_ref[...] = (keep_ref[:n, :].astype(F32) + pair_ref[:n, :].astype(F32)).astype(BF16)


def mixed_sum_kernel(keep_ref, pair_ref, cross_ref, out_ref):
    n = out_ref.shape[0]
    total = keep_ref[n:, :].astype(F32) + pair_ref[n:, :].astype(F32) + cross_ref[...].astype(F32)
    out_ref[...] = total.astype(BF16)


def call(kernel, name, out_shape, args, scratch=(), smem=0, hbm=0, us=1.0, vmem_mb=24):
    vmem = pl.BlockSpec(memory_space=pltpu.VMEM)
    return pl.pallas_call(
        kernel,
        out_shape=out_shape,
        in_specs=[pl.BlockSpec(memory_space=pltpu.SMEM)] * smem
        + [pl.BlockSpec(memory_space=pltpu.HBM)] * hbm
        + [vmem] * (len(args) - smem - hbm),
        out_specs=jax.tree.map(lambda _: vmem, out_shape),
        scratch_shapes=list(scratch),
        compiler_params=pltpu.CompilerParams(vmem_limit_bytes=vmem_mb * 2**20),
        cost_estimate=pl.CostEstimate(flops=int(us * 1e9), bytes_accessed=0, transcendentals=0),
        name=name,
    )(*args)


def local(queries, keys, values, w_out, d_out, lengths):
    tok, heads, hd = queries.shape
    width = w_out.shape[2]
    ctx = lax.axis_size(CTX)
    longest = tok * ctx * 5 // 8
    reach = min(ctx - 1, -(-(longest - 1) // tok))
    n_kv = reach + 1
    split = min(n_kv, 4)
    scale = hd ** (-0.5)
    quarter = tok // 4
    n_tensor = lax.axis_size("tensor")
    shape = jax.ShapeDtypeStruct

    def swap(x, mask):
        return lax.ppermute(x, "tensor", [(i, i ^ mask) for i in range(n_tensor)])

    def shift(x, d):
        pairs = [(i, i + d) for i in range(ctx - d)] if d > 0 else [(i - d, i) for i in range(ctx + d)]
        return lax.ppermute(x, CTX, pairs)

    begin = call(begin_kernel, "begin", shape((1, tok), jnp.int32), (lengths,), smem=1, us=6.0)
    keys, values, begin = lax.optimization_barrier((keys, values, begin))
    kv = jnp.concatenate([keys.reshape(tok, hd), values.reshape(tok, hd)], axis=1)
    w = w_out.reshape(heads * hd, width)
    pair = swap(d_out, 1)
    cross = swap(d_out, 2)
    kvs = [kv] + [shift(kv, d) for d in range(1, split)]
    kv_later, pair, queries, kvs[1] = lax.optimization_barrier((kv, pair, queries, kvs[1]))
    q = queries.transpose(1, 0, 2).reshape(heads * tok, hd)
    kvs += [shift(kv_later, d) for d in range(split, n_kv)]
    near, far = list(range(split)), list(range(split, n_kv))
    half_rows = pltpu.VMEM((tok // 2, width), BF16)
    d_near = call(
        d_attn_kernel, "d_attn_near", shape((tok // 2, heads * hd), BF16), (d_out, pair, w), scratch=(half_rows,), us=2.0
    )
    q, d_near = lax.optimization_barrier((q, d_near))
    row = shape((1, heads * tok), F32)
    state = (row, row, shape((hd, heads * tok), F32))
    held = pltpu.VMEM((split if split > UNROLL else 1, tok, 2 * hd), BF16)

    def blocks_of(group):
        return tuple(kvs[d] for d in group)

    begun = call(
        functools.partial(forward_kernel, near, heads, scale),
        "forward_near",
        state,
        (lengths, begin, q, *blocks_of(near)),
        scratch=(held,),
        smem=1,
        us=0.2,
    )
    attn, lse = call(
        functools.partial(forward_kernel, far, heads, scale),
        "forward_far",
        (shape((tok, heads * hd), BF16), row),
        (lengths, begin, q, *blocks_of(far), *begun),
        scratch=(held,) + tuple(pltpu.VMEM(x.shape, F32) for x in state),
        smem=1,
        us=5.0,
    )
    diag = swap(cross, 1)
    send, keep, g, delta = call(
        functools.partial(middle_kernel, heads),
        "middle",
        (shape((tok // 2, width), BF16),) * 2 + (shape((heads * tok, hd), BF16), row),
        (attn, d_near, cross, diag, w),
        scratch=(pltpu.VMEM((tok, heads * hd), BF16), half_rows),
        us=3.0,
    )
    from_pair = swap(send, 1)
    term = shape((tok, 2 * hd), BF16)

    def backward(blocks, name, us, dq=None, last=False):
        dq, *terms = call(
            functools.partial(backward_kernel, blocks, dq is None, last, heads, scale),
            name,
            (shape((tok, heads * hd), BF16) if last else state[2],) + (term,) * len(blocks),
            (lengths, begin, q, *blocks_of(blocks), g, lse, delta) + (() if dq is None else (dq,)),
            scratch=(held, held) + ((pltpu.VMEM(state[2].shape, F32),) if last else ()),
            smem=1,
            us=us,
        )
        return dq, dict(zip(blocks, terms))

    dq, terms = backward(near[1:], "backward_near", 3.0)
    from_pair, dq = lax.optimization_barrier((from_pair, dq))
    back = {d: shift(terms[d], -d) for d in reversed(near[1:])}
    to_cross = call(pair_sum_kernel, "pair_sum", shape((quarter, width), BF16), (keep, from_pair), us=0.5)
    from_cross = swap(to_cross, 2)
    dq, to_cross = lax.optimization_barrier((dq, to_cross))
    dq, terms = backward(far, "backward_far", 3.0, dq)
    back.update({d: shift(terms[d], -d) for d in far})
    dq, terms = backward([0], "backward_own", 2.0, dq, True)
    back = [terms[0]] + [back[d] for d in range(1, n_kv)]
    mixed = call(mixed_sum_kernel, "mixed_sum", shape((quarter, width), BF16), (keep, from_pair, from_cross), us=0.5)
    back[0], mixed = lax.optimization_barrier((back[0], mixed))
    dk, dv = call(
        functools.partial(finish_kernel, n_kv),
        "finish",
        (shape((tok, hd), BF16),) * 2,
        tuple(back),
        scratch=(pltpu.VMEM((n_kv, tok, 2 * hd), BF16), pltpu.SemaphoreType.DMA((n_kv,))),
        hbm=n_kv,
        us=0.5,
        vmem_mb=60,
    )
    return (mixed, dq.reshape(tok, heads, hd), dk.reshape(tok, 1, hd), dv.reshape(tok, 1, hd))


def solution(mesh):
    return jax.shard_map(
        local,
        mesh=mesh,
        in_specs=(
            P(("outer", "inner"), "tensor", None),
            P(("outer", "inner"), "tensor", None),
            P(("outer", "inner"), "tensor", None),
            P("tensor", None, None),
            P(("outer", "inner", "tensor"), None),
            P(),
        ),
        out_specs=(
            P(("outer", "inner", "tensor"), None),
            P(("outer", "inner"), "tensor", None),
            P(("outer", "inner"), "tensor", None),
            P(("outer", "inner"), "tensor", None),
        ),
        check_vma=False,
    )
```

time: 67.4 us -> 58.4 us (0.87)
  the two profiles are of different devices: /device:TPU:2 before, /device:TPU:0 now
where the time goes in v3:
time: 58.4 us; the launch traced here: 57.6 us
  starting transfers between devices  24.7 us (42%)
  waiting for transfers between devices  16.8 us (29%)
  Pallas kernels  12.8 us (22%)
  local copies, waits for them, and re-layouts  2.38 us (4%)
  between operations  0.93 us (2%)
    ppermute x10, starting transfers between devices, shift(): return lax.ppermute(x, CTX, pairs)  20.8 us
    pallas_call x11, Pallas kernels, call(): pl.pallas_call(kernel, out_shape=out_shape, in_specs=[pl.BlockSpec(memory...  12.8 us
    ppermute x5, waiting for transfers between devices, swap(): return lax.ppermute(x, 'tensor', [(i, i ^ mask) for i in range(n_tensor)])  9.66 us
    ppermute x10, waiting for transfers between devices, shift(): return lax.ppermute(x, CTX, pairs)  7.15 us
    ppermute x5, starting transfers between devices, swap(): return lax.ppermute(x, 'tensor', [(i, i ^ mask) for i in range(n_tensor)])  3.83 us
    unnamed x16, local copies, waits for them, and re-layouts  1.58 us
  transfers between devices with their start and end apart: 15, of which 4 were waited for; matrix products, arithmetic and copies ran while one was open for 1% of the time, Pallas kernels for 14%

profile of v3, /device:TPU:0, one launch (start us, length us, event | category | flops | bytes accessed | tf_op | source)
XLA Modules:
  0.0 57.6 jit_solution(16684433504791306964)
XLA Ops:
  0.6 0.5 collective-permute-start
  1.1 2.6 %collective-permute-start.6 = (bf16[64,4096]{1,0:T(8,128)(2,1)}, bf16[64,4096]{1,0:T(8,128)(2,1)S(1)}, u32[]{:S(2)}, u32[]{:S(2)}) collective-permute-start(bf16[64,4096]{1,0:T(8,128)(2,1)} %own_ref.1), channel_id=1, source_target_pairs={{0,2},{1,3},{2,0},{3,1},{4,6},{5,7},{6,4},{7,5},{8,10},{9,11},{10,... | collective-permute-start | bytes 1572872 | tf_op jit(solution)/shard_map/ppermute | solution.py:259
  3.7 0.7 %copy-done = s32[16]{0:T(128)S(1)} copy-done((s32[16]{0:T(128)S(1)}, s32[16]{0:T(128)}, u32[]{:S(2)}) %copy-start) | copy-done | bytes 88
  4.4 0.6 begin.1.begin_ref
  5.0 0.2 copy-done.6
  5.3 3.6 %collective-permute-start.1 = (bf16[256,256]{1,0:T(8,128)(2,1)S(1)}, bf16[256,256]{1,0:T(8,128)(2,1)S(1)}, u32[]{:S(2)}, u32[]{:S(2)}) collective-permute-start(bf16[256,256]{1,0:T(8,128)(2,1)S(1)} %pad_maximum_fusion.refs_0_), channel_id=1, source_target_pairs={{0,4},{4,8},{8,12},{12,16},{16,20},{20,24},{24,28},{1,5},{5,9},{9,... | collective-permute-start | bytes 393224 | tf_op jit(solution)/shard_map/ppermute | solution.py:263
  8.9 5.1 %collective-permute-start.5 = (bf16[256,256]{1,0:T(8,128)(2,1)S(1)}, bf16[256,256]{1,0:T(8,128)(2,1)S(1)}, u32[]{:S(2)}, u32[]{:S(2)}) collective-permute-start(bf16[256,256]{1,0:T(8,128)(2,1)S(1)} %pad_maximum_fusion.refs_0_), channel_id=1, source_target_pairs={{0,12},{4,16},{8,20},{12,24},{16,28},{1,13},{5,17},{9,21},{13,25},... | collective-permute-start | bytes 393224 | tf_op jit(solution)/shard_map/ppermute | solution.py:263
  14.0 2.7 %collective-permute-start.4 = (bf16[256,256]{1,0:T(8,128)(2,1)S(1)}, bf16[256,256]{1,0:T(8,128)(2,1)S(1)}, u32[]{:S(2)}, u32[]{:S(2)}) collective-permute-start(bf16[256,256]{1,0:T(8,128)(2,1)S(1)} %pad_maximum_fusion.refs_0_), channel_id=1, source_target_pairs={{0,8},{4,12},{8,16},{12,20},{16,24},{20,28},{1,9},{5,13},{9,17},{1... | collective-permute-start | bytes 393224 | tf_op jit(solution)/shard_map/ppermute | solution.py:263
  16.7 1.3 %collective-permute-start.3 = (bf16[256,256]{1,0:T(8,128)(2,1)S(1)}, bf16[256,256]{1,0:T(8,128)(2,1)S(1)}, u32[]{:S(2)}, u32[]{:S(2)}) collective-permute-start(bf16[256,256]{1,0:T(8,128)(2,1)S(1)} %pad_maximum_fusion.refs_0_), channel_id=1, source_target_pairs={{0,20},{4,24},{8,28},{1,21},{5,25},{9,29},{2,22},{6,26},{10,30},{3... | collective-permute-start | bytes 393224 | tf_op jit(solution)/shard_map/ppermute | solution.py:263
  18.0 1.7 %collective-permute-start.2 = (bf16[256,256]{1,0:T(8,128)(2,1)S(1)}, bf16[256,256]{1,0:T(8,128)(2,1)S(1)}, u32[]{:S(2)}, u32[]{:S(2)}) collective-permute-start(bf16[256,256]{1,0:T(8,128)(2,1)S(1)} %pad_maximum_fusion.refs_0_), channel_id=1, source_target_pairs={{0,16},{4,20},{8,24},{12,28},{1,17},{5,21},{9,25},{13,29},{2,18},{... | collective-permute-start | bytes 393224 | tf_op jit(solution)/shard_map/ppermute | solution.py:263
  19.9 1.5 %d_attn_near.1.near_ref = bf16[128,512]{1,0:T(8,128)(2,1)S(1)} custom-call(bf16[64,4096]{1,0:T(8,128)(2,1)S(1)} %copy-done.3, bf16[64,4096]{1,0:T(8,128)(2,1)S(1)} %collective-permute-done.pair_ref, bf16[512,4096]{1,0:T(8,128)(2,1)S(1)} %bitcast.12), custom_call_target="tpu_custom_call" | custom-call | flops 2000000000 | tf_op jit(solution)/shard_map/d_attn_near/pallas_call | solution.py:231
  21.5 1.3 %forward_near.1 = (f32[1,1024]{1,0:T(1,128)S(1)}, f32[1,1024]{1,0:T(1,128)S(1)}, f32[128,1024]{1,0:T(8,128)S(1)}) custom-call(s32[16]{0:T(128)S(1)} %copy-done.1, s32[1,256]{1,0:T(1,128)S(1)} %begin.1.begin_ref, bf16[1024,128]{1,0:T(8,128)(2,1)S(1)} %bitcast.7, bf16[256,256]{1,0:T(8,128)(2,1)S(1)} %pad_maximum_fusion.refs_0_, ...), custom_call_target="tpu_custom_call" | custom-call | flops 200000000 | tf_op jit(solution)/shard_map/forward_near/pallas_call | solution.py:231
  22.8 1.5 %collective-permute-done.2.refs_0_ = bf16[256,256]{1,0:T(8,128)(2,1)S(1)} collective-permute-done((bf16[256,256]{1,0:T(8,128)(2,1)S(1)}, bf16[256,256]{1,0:T(8,128)(2,1)S(1)}, u32[]{:S(2)}, u32[]{:S(2)}) %collective-permute-start.2) | collective-permute-done | bytes 131104 | tf_op jit(solution)/shard_map/ppermute | solution.py:263
  24.3 0.7 %forward_far.1 = (bf16[256,512]{1,0:T(8,128)(2,1)S(1)}, f32[1,1024]{1,0:T(1,128)S(1)}) custom-call(s32[16]{0:T(128)S(1)} %copy-done.1, s32[1,256]{1,0:T(1,128)S(1)} %begin.1.begin_ref, bf16[1024,128]{1,0:T(8,128)(2,1)S(1)} %bitcast.8, bf16[256,256]{1,0:T(8,128)(2,1)S(1)} %collective-permute-done.2.refs_0_, ...), custom_call_target="tpu_custom_call" | custom-call | flops 5000000000 | tf_op jit(solution)/shard_map/forward_far/pallas_call | solution.py:231
  25.1 2.9 %middle.1 = (bf16[128,4096]{1,0:T(8,128)(2,1)S(1)}, bf16[128,4096]{1,0:T(8,128)(2,1)S(1)}, bf16[1024,128]{1,0:T(8,128)(2,1)S(1)}, f32[1,1024]{1,0:T(1,128)S(1)}) custom-call(bf16[256,512]{1,0:T(8,128)(2,1)S(1)} %get-tuple-element.49.attn_ref, bf16[128,512]{1,0:T(8,128)(2,1)S(1)} %d_attn_near.1.near_ref, ...), custom_call_target="tpu_custom_call" | custom-call | flops 3000000000 | tf_op jit(solution)/shard_map/middle/pallas_call | solution.py:231
  28.0 0.6 %backward_near.1 = (f32[128,1024]{1,0:T(8,128)S(1)}, bf16[256,256]{1,0:T(8,128)(2,1)S(1)}, bf16[256,256]{1,0:T(8,128)(2,1)S(1)}, bf16[256,256]{1,0:T(8,128)(2,1)S(1)}) custom-call(s32[16]{0:T(128)S(1)} %copy-done.1, s32[1,256]{1,0:T(1,128)S(1)} %begin.1.begin_ref, bf16[1024,128]{1,0:T(8,128)(2,1)S(1)} %bitcast.9, ...), custom_call_target="tpu_custom_call" | custom-call | flops 3000000000 | tf_op jit(solution)/shard_map/backward_near/pallas_call | solution.py:231
  28.6 2.0 %collective-permute-done.8.pair_ref = bf16[128,4096]{1,0:T(8,128)(2,1)S(1)} collective-permute-done((bf16[128,4096]{1,0:T(8,128)(2,1)S(1)}, bf16[128,4096]{1,0:T(8,128)(2,1)S(1)}, u32[]{:S(2)}, u32[]{:S(2)}) %collective-permute-start.8) | collective-permute-done | bytes 1048608 | tf_op jit(solution)/shard_map/ppermute | solution.py:259
  30.7 0.1 pair_sum.1
  30.8 0.6 collective-permute-start.9
  31.4 1.3 %collective-permute-start.10 = (bf16[256,256]{1,0:T(8,128)(2,1)S(1)}, bf16[256,256]{1,0:T(8,128)(2,1)}, u32[]{:S(2)}, u32[]{:S(2)}) collective-permute-start(bf16[256,256]{1,0:T(8,128)(2,1)S(1)} %get-tuple-element.65), channel_id=1, source_target_pairs={{4,0},{8,4},{12,8},{16,12},{20,16},{24,20},{28,24},{5,1},{9,5},{13... | collective-permute-start | bytes 393224 | tf_op jit(solution)/shard_map/ppermute | solution.py:263
  32.6 1.3 %collective-permute-start.11 = (bf16[256,256]{1,0:T(8,128)(2,1)S(1)}, bf16[256,256]{1,0:T(8,128)(2,1)}, u32[]{:S(2)}, u32[]{:S(2)}) collective-permute-start(bf16[256,256]{1,0:T(8,128)(2,1)S(1)} %get-tuple-element.66), channel_id=1, source_target_pairs={{8,0},{12,4},{16,8},{20,12},{24,16},{28,20},{9,1},{13,5},{17,9},{2... | collective-permute-start | bytes 393224 | tf_op jit(solution)/shard_map/ppermute | solution.py:263
  33.9 1.3 %collective-permute-start.12 = (bf16[256,256]{1,0:T(8,128)(2,1)S(1)}, bf16[256,256]{1,0:T(8,128)(2,1)}, u32[]{:S(2)}, u32[]{:S(2)}) collective-permute-start(bf16[256,256]{1,0:T(8,128)(2,1)S(1)} %get-tuple-element.67), channel_id=1, source_target_pairs={{12,0},{16,4},{20,8},{24,12},{28,16},{13,1},{17,5},{21,9},{25,13},... | collective-permute-start | bytes 393224 | tf_op jit(solution)/shard_map/ppermute | solution.py:263
  35.2 0.6 %backward_far.1 = (f32[128,1024]{1,0:T(8,128)S(1)}, bf16[256,256]{1,0:T(8,128)(2,1)S(1)}, bf16[256,256]{1,0:T(8,128)(2,1)S(1)}) custom-call(s32[16]{0:T(128)S(1)} %copy-done.1, s32[1,256]{1,0:T(1,128)S(1)} %begin.1.begin_ref, bf16[1024,128]{1,0:T(8,128)(2,1)S(1)} %bitcast.10, bf16[256,256]{1,0:T(8,128)(2,1)S(1)} %collective-permute-done.2.refs_0_, ...), custom_call_target="tpu_custom_call" | custom-call | flops 3000000000 | tf_op jit(solution)/shard_map/backward_far/pallas_call | solution.py:231
  35.9 1.3 %collective-permute-start.13 = (bf16[256,256]{1,0:T(8,128)(2,1)S(1)}, bf16[256,256]{1,0:T(8,128)(2,1)}, u32[]{:S(2)}, u32[]{:S(2)}) collective-permute-start(bf16[256,256]{1,0:T(8,128)(2,1)S(1)} %get-tuple-element.68), channel_id=1, source_target_pairs={{16,0},{20,4},{24,8},{28,12},{17,1},{21,5},{25,9},{29,13},{18,2},{... | collective-permute-start | bytes 393224 | tf_op jit(solution)/shard_map/ppermute | solution.py:263
  37.2 7.6 %collective-permute-done.9.cross_ref = bf16[64,4096]{1,0:T(8,128)(2,1)S(1)} collective-permute-done((bf16[64,4096]{1,0:T(8,128)(2,1)S(1)}, bf16[64,4096]{1,0:T(8,128)(2,1)S(1)}, u32[]{:S(2)}, u32[]{:S(2)}) %collective-permute-start.9) | collective-permute-done | bytes 524320 | tf_op jit(solution)/shard_map/ppermute | solution.py:259
  44.8 1.3 %collective-permute-start.14 = (bf16[256,256]{1,0:T(8,128)(2,1)S(1)}, bf16[256,256]{1,0:T(8,128)(2,1)}, u32[]{:S(2)}, u32[]{:S(2)}) collective-permute-start(bf16[256,256]{1,0:T(8,128)(2,1)S(1)} %get-tuple-element.69), channel_id=1, source_target_pairs={{20,0},{24,4},{28,8},{21,1},{25,5},{29,9},{22,2},{26,6},{30,10},{2... | collective-permute-start | bytes 393224 | tf_op jit(solution)/shard_map/ppermute | solution.py:263
  46.1 1.5 %backward_own.1 = (bf16[256,512]{1,0:T(8,128)(2,1)S(1)}, bf16[256,256]{1,0:T(8,128)(2,1)S(1)}) custom-call(s32[16]{0:T(128)S(1)} %copy-done.1, s32[1,256]{1,0:T(1,128)S(1)} %begin.1.begin_ref, bf16[1024,128]{1,0:T(8,128)(2,1)S(1)} %bitcast.11, bf16[256,256]{1,0:T(8,128)(2,1)S(1)} %pad_maximum_fusion.refs_0_, ...), custom_call_target="tpu_custom_call" | custom-call | flops 2000000000 | tf_op jit(solution)/shard_map/backward_own/pallas_call | solution.py:231
  47.6 0.6 %copy-done.4 = bf16[256,256]{1,0:T(8,128)(2,1)} copy-done((bf16[256,256]{1,0:T(8,128)(2,1)}, bf16[256,256]{1,0:T(8,128)(2,1)S(1)}, u32[]{:S(2)}) %copy-start.4) | copy-done | bytes 131096
  48.3 0.8 %reshape.33 = bf16[256,4,128]{2,1,0:T(4,128)(2,1)} reshape(bf16[256,512]{1,0:T(8,128)(2,1)S(1)} %get-tuple-element.63) | data formatting | bytes 524288 | tf_op jit(solution)/shard_map/reshape | solution.py:352
  49.1 1.0 %mixed_sum.1 = bf16[64,4096]{1,0:T(8,128)(2,1)} custom-call(bf16[128,4096]{1,0:T(8,128)(2,1)S(1)} %get-tuple-element.57.keep_ref, bf16[128,4096]{1,0:T(8,128)(2,1)S(1)} %collective-permute-done.8.pair_ref, bf16[64,4096]{1,0:T(8,128)(2,1)S(1)} %collective-permute-done.9.cross_ref), custom_call_target="tpu_custom_call" | custom-call | flops 500000000 | tf_op jit(solution)/shard_map/mixed_sum/pallas_call | solution.py:231
  50.1 5.6 %collective-permute-done.14.refs_5_ = bf16[256,256]{1,0:T(8,128)(2,1)} collective-permute-done((bf16[256,256]{1,0:T(8,128)(2,1)S(1)}, bf16[256,256]{1,0:T(8,128)(2,1)}, u32[]{:S(2)}, u32[]{:S(2)}) %collective-permute-start.14) | collective-permute-done | bytes 131104 | tf_op jit(solution)/shard_map/ppermute | solution.py:263
  55.7 2.0 %finish.1 = (bf16[256,128]{1,0:T(8,128)(2,1)}, bf16[256,128]{1,0:T(8,128)(2,1)}) custom-call(bf16[256,256]{1,0:T(8,128)(2,1)} %copy-done.4, bf16[256,256]{1,0:T(8,128)(2,1)} %collective-permute-done.10.refs_1_, bf16[256,256]{1,0:T(8,128)(2,1)} %collective-permute-done.11.refs_2_, bf16[256,256]{1,0:T(8,128)(2,1)} %collective-permute-done.12.refs_3_, ...), custom_call_target="tpu_custom_call" | custom-call | flops 500000000 | tf_op jit(solution)/shard_map/finish/pallas_call | solution.py:231
  (28 shorter events, 0.3 us)
Async XLA Ops:
  0.6 16.1 %collective-permute-start = (bf16[64,4096]{1,0:T(8,128)(2,1)}, bf16[64,4096]{1,0:T(8,128)(2,1)S(1)}, u32[]{:S(2)}, u32[]{:S(2)}) collective-permute-start(bf16[64,4096]{1,0:T(8,128)(2,1)} %own_ref.1), channel_id=1, source_target_pairs={{0,1},{1,0},{2,3},{3,2},{4,5},{5,4},{6,7},{7,6},{8,9},{9,8},{10,11... | collective-permute-start | bytes 1572872 | tf_op jit(solution)/shard_map/ppermute | solution.py:259
  1.1 18.6 %collective-permute-start.6 = (bf16[64,4096]{1,0:T(8,128)(2,1)}, bf16[64,4096]{1,0:T(8,128)(2,1)S(1)}, u32[]{:S(2)}, u32[]{:S(2)}) collective-permute-start(bf16[64,4096]{1,0:T(8,128)(2,1)} %own_ref.1), channel_id=1, source_target_pairs={{0,2},{1,3},{2,0},{3,1},{4,6},{5,7},{6,4},{7,5},{8,10},{9,11},{10,... | collective-permute-start | bytes 1572872 | tf_op jit(solution)/shard_map/ppermute | solution.py:259
  3.7 0.7 %copy-start = (s32[16]{0:T(128)S(1)}, s32[16]{0:T(128)}, u32[]{:S(2)}) copy-start(s32[16]{0:T(128)} %len_ref.11) | copy-start | bytes 196
  4.4 0.8 %copy-start.6 = (bf16[256,1,128]{2,0,1:T(8,128)(2,1)S(1)}, bf16[256,1,128]{2,0,1:T(8,128)(2,1)}, u32[]{:S(2)}) copy-start(bf16[256,1,128]{2,0,1:T(8,128)(2,1)} %param.8) | copy-start | bytes 196612
  4.4 0.9 %copy-start.7 = (bf16[256,1,128]{2,0,1:T(8,128)(2,1)S(1)}, bf16[256,1,128]{2,0,1:T(8,128)(2,1)}, u32[]{:S(2)}) copy-start(bf16[256,1,128]{2,0,1:T(8,128)(2,1)} %param.7) | copy-start | bytes 196612
  4.4 15.4 %copy-start.2 = (bf16[4,128,4096]{2,1,0:T(8,128)(2,1)S(1)}, bf16[4,128,4096]{2,1,0:T(8,128)(2,1)}, u32[]{:S(2)}) copy-start(bf16[4,128,4096]{2,1,0:T(8,128)(2,1)} %param.9) | copy-start | bytes 12582916
  4.4 15.5 %copy-start.3 = (bf16[64,4096]{1,0:T(8,128)(2,1)S(1)}, bf16[64,4096]{1,0:T(8,128)(2,1)}, u32[]{:S(2)}) copy-start(bf16[64,4096]{1,0:T(8,128)(2,1)} %own_ref.1) | copy-start | bytes 1572868
  5.0 16.4 %copy-start.5 = (bf16[256,4,128]{2,1,0:T(4,128)(2,1)S(1)}, bf16[256,4,128]{2,1,0:T(4,128)(2,1)}, u32[]{:S(2)}) copy-start(bf16[256,4,128]{2,1,0:T(4,128)(2,1)} %param.6) | copy-start | bytes 786436
  5.0 16.5 %copy-start.1 = (s32[16]{0:T(128)S(1)}, s32[16]{0:T(128)}, u32[]{:S(2)}) copy-start(s32[16]{0:T(128)} %len_ref.11) | copy-start | bytes 196
  5.3 11.4 %collective-permute-start.1 = (bf16[256,256]{1,0:T(8,128)(2,1)S(1)}, bf16[256,256]{1,0:T(8,128)(2,1)S(1)}, u32[]{:S(2)}, u32[]{:S(2)}) collective-permute-start(bf16[256,256]{1,0:T(8,128)(2,1)S(1)} %pad_maximum_fusion.refs_0_), channel_id=1, source_target_pairs={{0,4},{4,8},{8,12},{12,16},{16,20},{20,24},{24,28},{1,5},{5,9},{9,... | collective-permute-start | bytes 393224 | tf_op jit(solution)/shard_map/ppermute | solution.py:263
  8.9 12.5 %collective-permute-start.5 = (bf16[256,256]{1,0:T(8,128)(2,1)S(1)}, bf16[256,256]{1,0:T(8,128)(2,1)S(1)}, u32[]{:S(2)}, u32[]{:S(2)}) collective-permute-start(bf16[256,256]{1,0:T(8,128)(2,1)S(1)} %pad_maximum_fusion.refs_0_), channel_id=1, source_target_pairs={{0,12},{4,16},{8,20},{12,24},{16,28},{1,13},{5,17},{9,21},{13,25},... | collective-permute-start | bytes 393224 | tf_op jit(solution)/shard_map/ppermute | solution.py:263
  14.0 7.5 %collective-permute-start.4 = (bf16[256,256]{1,0:T(8,128)(2,1)S(1)}, bf16[256,256]{1,0:T(8,128)(2,1)S(1)}, u32[]{:S(2)}, u32[]{:S(2)}) collective-permute-start(bf16[256,256]{1,0:T(8,128)(2,1)S(1)} %pad_maximum_fusion.refs_0_), channel_id=1, source_target_pairs={{0,8},{4,12},{8,16},{12,20},{16,24},{20,28},{1,9},{5,13},{9,17},{1... | collective-permute-start | bytes 393224 | tf_op jit(solution)/shard_map/ppermute | solution.py:263
  16.7 6.1 %collective-permute-start.3 = (bf16[256,256]{1,0:T(8,128)(2,1)S(1)}, bf16[256,256]{1,0:T(8,128)(2,1)S(1)}, u32[]{:S(2)}, u32[]{:S(2)}) collective-permute-start(bf16[256,256]{1,0:T(8,128)(2,1)S(1)} %pad_maximum_fusion.refs_0_), channel_id=1, source_target_pairs={{0,20},{4,24},{8,28},{1,21},{5,25},{9,29},{2,22},{6,26},{10,30},{3... | collective-permute-start | bytes 393224 | tf_op jit(solution)/shard_map/ppermute | solution.py:263
  18.0 6.3 %collective-permute-start.2 = (bf16[256,256]{1,0:T(8,128)(2,1)S(1)}, bf16[256,256]{1,0:T(8,128)(2,1)S(1)}, u32[]{:S(2)}, u32[]{:S(2)}) collective-permute-start(bf16[256,256]{1,0:T(8,128)(2,1)S(1)} %pad_maximum_fusion.refs_0_), channel_id=1, source_target_pairs={{0,16},{4,20},{8,24},{12,28},{1,17},{5,21},{9,25},{13,29},{2,18},{... | collective-permute-start | bytes 393224 | tf_op jit(solution)/shard_map/ppermute | solution.py:263
  19.8 5.3 %collective-permute-start.7 = (bf16[64,4096]{1,0:T(8,128)(2,1)S(1)}, bf16[64,4096]{1,0:T(8,128)(2,1)S(1)}, u32[]{:S(2)}, u32[]{:S(2)}) collective-permute-start(bf16[64,4096]{1,0:T(8,128)(2,1)S(1)} %collective-permute-done.6.cross_ref), channel_id=1, source_target_pairs={{0,1},{1,0},{2,3},{3,2},{4,5},{5,4},{6,7},{7,6},{8,9},{9,8},{10,11... | collective-permute-start | bytes 1572872 | tf_op jit(solution)/shard_map/ppermute | solution.py:259
  27.9 2.7 %collective-permute-start.8 = (bf16[128,4096]{1,0:T(8,128)(2,1)S(1)}, bf16[128,4096]{1,0:T(8,128)(2,1)S(1)}, u32[]{:S(2)}, u32[]{:S(2)}) collective-permute-start(bf16[128,4096]{1,0:T(8,128)(2,1)S(1)} %get-tuple-element.54), channel_id=1, source_target_pairs={{0,1},{1,0},{2,3},{3,2},{4,5},{5,4},{6,7},{7,6},{8,9},{9,8},{10,11... | collective-permute-start | bytes 3145736 | tf_op jit(solution)/shard_map/ppermute | solution.py:259
  30.8 14.0 %collective-permute-start.9 = (bf16[64,4096]{1,0:T(8,128)(2,1)S(1)}, bf16[64,4096]{1,0:T(8,128)(2,1)S(1)}, u32[]{:S(2)}, u32[]{:S(2)}) collective-permute-start(bf16[64,4096]{1,0:T(8,128)(2,1)S(1)} %pair_sum.1), channel_id=1, source_target_pairs={{0,2},{1,3},{2,0},{3,1},{4,6},{5,7},{6,4},{7,5},{8,10},{9,11},{10,... | collective-permute-start | bytes 1572872 | tf_op jit(solution)/shard_map/ppermute | solution.py:259
  31.4 18.7 %collective-permute-start.10 = (bf16[256,256]{1,0:T(8,128)(2,1)S(1)}, bf16[256,256]{1,0:T(8,128)(2,1)}, u32[]{:S(2)}, u32[]{:S(2)}) collective-permute-start(bf16[256,256]{1,0:T(8,128)(2,1)S(1)} %get-tuple-element.65), channel_id=1, source_target_pairs={{4,0},{8,4},{12,8},{16,12},{20,16},{24,20},{28,24},{5,1},{9,5},{13... | collective-permute-start | bytes 393224 | tf_op jit(solution)/shard_map/ppermute | solution.py:263
  32.6 17.4 %collective-permute-start.11 = (bf16[256,256]{1,0:T(8,128)(2,1)S(1)}, bf16[256,256]{1,0:T(8,128)(2,1)}, u32[]{:S(2)}, u32[]{:S(2)}) collective-permute-start(bf16[256,256]{1,0:T(8,128)(2,1)S(1)} %get-tuple-element.66), channel_id=1, source_target_pairs={{8,0},{12,4},{16,8},{20,12},{24,16},{28,20},{9,1},{13,5},{17,9},{2... | collective-permute-start | bytes 393224 | tf_op jit(solution)/shard_map/ppermute | solution.py:263
  33.9 16.1 %collective-permute-start.12 = (bf16[256,256]{1,0:T(8,128)(2,1)S(1)}, bf16[256,256]{1,0:T(8,128)(2,1)}, u32[]{:S(2)}, u32[]{:S(2)}) collective-permute-start(bf16[256,256]{1,0:T(8,128)(2,1)S(1)} %get-tuple-element.67), channel_id=1, source_target_pairs={{12,0},{16,4},{20,8},{24,12},{28,16},{13,1},{17,5},{21,9},{25,13},... | collective-permute-start | bytes 393224 | tf_op jit(solution)/shard_map/ppermute | solution.py:263
  35.9 14.2 %collective-permute-start.13 = (bf16[256,256]{1,0:T(8,128)(2,1)S(1)}, bf16[256,256]{1,0:T(8,128)(2,1)}, u32[]{:S(2)}, u32[]{:S(2)}) collective-permute-start(bf16[256,256]{1,0:T(8,128)(2,1)S(1)} %get-tuple-element.68), channel_id=1, source_target_pairs={{16,0},{20,4},{24,8},{28,12},{17,1},{21,5},{25,9},{29,13},{18,2},{... | collective-permute-start | bytes 393224 | tf_op jit(solution)/shard_map/ppermute | solution.py:263
  44.8 10.8 %collective-permute-start.14 = (bf16[256,256]{1,0:T(8,128)(2,1)S(1)}, bf16[256,256]{1,0:T(8,128)(2,1)}, u32[]{:S(2)}, u32[]{:S(2)}) collective-permute-start(bf16[256,256]{1,0:T(8,128)(2,1)S(1)} %get-tuple-element.69), channel_id=1, source_target_pairs={{20,0},{24,4},{28,8},{21,1},{25,5},{29,9},{22,2},{26,6},{30,10},{2... | collective-permute-start | bytes 393224 | tf_op jit(solution)/shard_map/ppermute | solution.py:263
  47.6 0.7 %copy-start.4 = (bf16[256,256]{1,0:T(8,128)(2,1)}, bf16[256,256]{1,0:T(8,128)(2,1)S(1)}, u32[]{:S(2)}) copy-start(bf16[256,256]{1,0:T(8,128)(2,1)S(1)} %get-tuple-element.64.refs_0_) | copy-start | bytes 393220

commit v4 on v3

--- a/solution.py
+++ b/solution.py
@@ -72,12 +72,15 @@
     out_ref[...] = begin
 
 
-def d_attn_kernel(own_ref, pair_ref, w_ref, out_ref, rows):
-    core = lax.axis_index("tensor") & 1
+def d_attn_kernel(own_ref, pair_ref, cross_ref, diag_ref, w_ref, out_ref, rows):
+    t = lax.axis_index("tensor")
     quarter = own_ref.shape[0]
-    rows[pl.ds(pl.multiple_of(core * quarter, quarter), quarter), :] = own_ref[...]
-    rows[pl.ds(pl.multiple_of((1 - core) * quarter, quarter), quarter), :] = pair_ref[...]
-    out_ref[...] = dot_nt(rows[...], w_ref[...]).astype(BF16)
+    tok, hd = rows.shape[0], out_ref.shape[1]
+    for mask, ref in enumerate((own_ref, pair_ref, cross_ref, diag_ref)):
+        rows[pl.ds(pl.multiple_of((t ^ mask) * quarter, quarter), quarter), :] = ref[...]
+    d_attn = dot_nt(rows[...], w_ref[...]).astype(BF16)
+    for h in range(d_attn.shape[1] // hd):
+        out_ref[h * tok : (h + 1) * tok, :] = d_attn[:, h * hd : (h + 1) * hd]
 
 
 def forward_kernel(blocks, heads, scale, len_ref, begin_ref, q_ref, *refs):
@@ -121,10 +124,8 @@
         attn_ref[:, h * hd : (h + 1) * hd] = (acc[:, cols] / denom[:, cols]).T.astype(BF16)
 
 
-def middle_kernel(heads, attn_ref, near_ref, cross_ref, diag_ref, w_ref, *refs):
-    send_ref, keep_ref, g_ref, delta_ref, rows, others = refs
+def project_kernel(heads, attn_ref, g_ref, w_ref, send_ref, keep_ref, delta_ref, rows):
     t = lax.axis_index("tensor")
-    chip, core = t >> 1, t & 1
     tok = attn_ref.shape[0]
     hd = attn_ref.shape[1] // heads
     quarter, half = tok // 4, tok // 2
@@ -137,15 +138,9 @@
         mixed = dot_nn(rows[...], w_ref[:, cols]).astype(BF16)
         send_ref[:, cols] = mixed[:half, :]
         keep_ref[:, cols] = mixed[half:, :]
-    others[pl.ds(pl.multiple_of(core * quarter, quarter), quarter), :] = cross_ref[...]
-    others[pl.ds(pl.multiple_of((1 - core) * quarter, quarter), quarter), :] = diag_ref[...]
-    far = dot_nt(others[...], w_ref[...]).astype(BF16)
     for h in range(heads):
-        part = slice(h * hd, (h + 1) * hd)
-        g_ref[pl.ds(pl.multiple_of(h * tok + chip * half, half), half), :] = near_ref[:, part]
-        g_ref[pl.ds(pl.multiple_of(h * tok + (1 - chip) * half, half), half), :] = far[:, part]
         cols = slice(h * tok, (h + 1) * tok)
-        prod = g_ref[cols, :].astype(F32) * attn_ref[:, part].astype(F32)
+        prod = g_ref[cols, :].astype(F32) * attn_ref[:, h * hd : (h + 1) * hd].astype(F32)
         delta_ref[:, cols] = jnp.sum(prod.T, axis=0, keepdims=True)
 
 
@@ -262,22 +257,17 @@
         pairs = [(i, i + d) for i in range(ctx - d)] if d > 0 else [(i - d, i) for i in range(ctx + d)]
         return lax.ppermute(x, CTX, pairs)
 
-    begin = call(begin_kernel, "begin", shape((1, tok), jnp.int32), (lengths,), smem=1, us=6.0)
-    keys, values, begin = lax.optimization_barrier((keys, values, begin))
     kv = jnp.concatenate([keys.reshape(tok, hd), values.reshape(tok, hd)], axis=1)
     w = w_out.reshape(heads * hd, width)
     pair = swap(d_out, 1)
     cross = swap(d_out, 2)
     kvs = [kv] + [shift(kv, d) for d in range(1, split)]
-    kv_later, pair, queries, kvs[1] = lax.optimization_barrier((kv, pair, queries, kvs[1]))
+    kv_later, pair, queries, lengths, kvs[1] = lax.optimization_barrier((kv, pair, queries, lengths, kvs[1]))
+    begin = call(begin_kernel, "begin", shape((1, tok), jnp.int32), (lengths,), smem=1, us=0.2)
+    cross, begin = lax.optimization_barrier((cross, begin))
     q = queries.transpose(1, 0, 2).reshape(heads * tok, hd)
     kvs += [shift(kv_later, d) for d in range(split, n_kv)]
     near, far = list(range(split)), list(range(split, n_kv))
-    half_rows = pltpu.VMEM((tok // 2, width), BF16)
-    d_near = call(
-        d_attn_kernel, "d_attn_near", shape((tok // 2, heads * hd), BF16), (d_out, pair, w), scratch=(half_rows,), us=2.0
-    )
-    q, d_near = lax.optimization_barrier((q, d_near))
     row = shape((1, heads * tok), F32)
     state = (row, row, shape((hd, heads * tok), F32))
     held = pltpu.VMEM((split if split > UNROLL else 1, tok, 2 * hd), BF16)
@@ -292,8 +282,19 @@
         (lengths, begin, q, *blocks_of(near)),
         scratch=(held,),
         smem=1,
-        us=0.2,
-    )
+        us=6.0,
+    )
+    begun, d_out = lax.optimization_barrier((begun, d_out))
+    diag = swap(cross, 1)
+    g = call(
+        d_attn_kernel,
+        "d_attn",
+        shape((heads * tok, hd), BF16),
+        (d_out, pair, cross, diag, w),
+        scratch=(pltpu.VMEM((tok, width), BF16),),
+        us=2.0,
+    )
+    begun, g = lax.optimization_barrier((begun, g))
     attn, lse = call(
         functools.partial(forward_kernel, far, heads, scale),
         "forward_far",
@@ -303,14 +304,13 @@
         smem=1,
         us=5.0,
     )
-    diag = swap(cross, 1)
-    send, keep, g, delta = call(
-        functools.partial(middle_kernel, heads),
-        "middle",
-        (shape((tok // 2, width), BF16),) * 2 + (shape((heads * tok, hd), BF16), row),
-        (attn, d_near, cross, diag, w),
-        scratch=(pltpu.VMEM((tok, heads * hd), BF16), half_rows),
-        us=3.0,
+    send, keep, delta = call(
+        functools.partial(project_kernel, heads),
+        "project",
+        (shape((tok // 2, width), BF16),) * 2 + (row,),
+        (attn, g, w),
+        scratch=(pltpu.VMEM((tok, heads * hd), BF16),),
+        us=2.0,
     )
     from_pair = swap(send, 1)
     term = shape((tok, 2 * hd), BF16)
@@ -327,14 +327,19 @@
         )
         return dq, dict(zip(blocks, terms))
 
-    dq, terms = backward(near[1:], "backward_near", 3.0)
+    short = [1, lax.axis_size("inner")]
+    if n_kv > UNROLL or short[1] not in range(2, n_kv):
+        short = far
+    dq, terms = backward([d for d in range(1, n_kv) if d not in short], "backward_first", 3.0)
     from_pair, dq = lax.optimization_barrier((from_pair, dq))
-    back = {d: shift(terms[d], -d) for d in reversed(near[1:])}
+    back = {d: shift(terms[d], -d) for d in terms}
+    early = max(back)
     to_cross = call(pair_sum_kernel, "pair_sum", shape((quarter, width), BF16), (keep, from_pair), us=0.5)
     from_cross = swap(to_cross, 2)
     dq, to_cross = lax.optimization_barrier((dq, to_cross))
-    dq, terms = backward(far, "backward_far", 3.0, dq)
-    back.update({d: shift(terms[d], -d) for d in far})
+    dq, terms = backward(short, "backward_second", 3.0, dq)
+    terms[short[0]], back[early] = lax.optimization_barrier((terms[short[0]], back[early]))
+    back.update({d: shift(terms[d], -d) for d in short})
     dq, terms = backward([0], "backward_own", 2.0, dq, True)
     back = [terms[0]] + [back[d] for d in range(1, n_kv)]
     mixed = call(mixed_sum_kernel, "mixed_sum", shape((quarter, width), BF16), (keep, from_pair, from_cross), us=0.5)

time: 58.4 us -> 54.1 us (0.926)
  waiting for transfers between devices: 16.8 us -> 10.9 us
  local copies, waits for them, and re-layouts: 2.38 us -> 3.49 us
  other arithmetic: 0.02 us -> 0.89 us
    ppermute x5, waiting for transfers between devices: 9.66 us -> 1.6 us  [swap(): return lax.ppermute(x, 'tensor', [(i, i ^ mask) for i in range(n_tensor)])]
    ppermute x10, waiting for transfers between devices: 7.15 us -> 9.32 us  [shift(): return lax.ppermute(x, CTX, pairs)]
    transpose x1, local copies, waits for them, and re-layouts: 0.04 us -> 0.99 us  [local(): q = queries.transpose(1, 0, 2).reshape(heads * tok, hd)]
    concatenate x1, other arithmetic: 0.02 us -> 0.89 us  [local(): jnp.concatenate([keys.reshape(tok, hd), values.reshape(tok, hd)], axis=1)]
    unnamed x16 -> x12, local copies, waits for them, and re-layouts: 1.58 us -> 1.74 us
  transfers between devices with their start and end apart: 15 -> 15, of which waited for: 4 -> 5; matrix products, arithmetic and copies ran while one was open for 1% -> 5% of each run, Pallas kernels for 14% -> 16%
where the time goes in v4:
time: 54.1 us; the launch traced here: 53.7 us
  starting transfers between devices  25 us (46%)
  Pallas kernels  12.5 us (23%)
  waiting for transfers between devices  10.9 us (20%)
  local copies, waits for them, and re-layouts  3.49 us (6%)
  other arithmetic  0.89 us (2%)
  between operations  0.88 us (2%)
    ppermute x10, starting transfers between devices, shift(): return lax.ppermute(x, CTX, pairs)  20.7 us
    pallas_call x11, Pallas kernels, call(): pl.pallas_call(kernel, out_shape=out_shape, in_specs=[pl.BlockSpec(memory...  12.5 us
    ppermute x10, waiting for transfers between devices, shift(): return lax.ppermute(x, CTX, pairs)  9.32 us
    ppermute x5, starting transfers between devices, swap(): return lax.ppermute(x, 'tensor', [(i, i ^ mask) for i in range(n_tensor)])  4.32 us
    unnamed x12, local copies, waits for them, and re-layouts  1.74 us
    ppermute x5, waiting for transfers between devices, swap(): return lax.ppermute(x, 'tensor', [(i, i ^ mask) for i in range(n_tensor)])  1.6 us
  transfers between devices with their start and end apart: 15, of which 5 were waited for; matrix products, arithmetic and copies ran while one was open for 5% of the time, Pallas kernels for 16%

profile of v4, /device:TPU:0, one launch (start us, length us, event | category | flops | bytes accessed | tf_op | source)
XLA Modules:
  0.0 53.7 jit_solution(11924858801990895138)
XLA Ops:
  1.1 2.6 %collective-permute-start.2 = (bf16[64,4096]{1,0:T(8,128)(2,1)}, bf16[64,4096]{1,0:T(8,128)(2,1)S(1)}, u32[]{:S(2)}, u32[]{:S(2)}) collective-permute-start(bf16[64,4096]{1,0:T(8,128)(2,1)} %own_ref), channel_id=1, source_target_pairs={{0,2},{1,3},{2,0},{3,1},{4,6},{5,7},{6,4},{7,5},{8,10},{9,11},{10,... | collective-permute-start | bytes 1572872 | tf_op jit(solution)/shard_map/ppermute | solution.py:254
  3.7 0.9 %pad_maximum_fusion.refs_0_ = bf16[256,256]{1,0:T(8,128)(2,1)S(1)} fusion(bf16[256,128]{1,0:T(8,128)(2,1)} %bitcast.15, bf16[256,128]{1,0:T(8,128)(2,1)} %bitcast.16), kind=kLoop, calls=%fused_computation | loop fusion | flops 262144 | bytes 262144 | tf_op jit(solution)/shard_map/concatenate | solution.py:260
  4.6 3.5 %collective-permute-start.1 = (bf16[256,256]{1,0:T(8,128)(2,1)S(1)}, bf16[256,256]{1,0:T(8,128)(2,1)S(1)}, u32[]{:S(2)}, u32[]{:S(2)}) collective-permute-start(bf16[256,256]{1,0:T(8,128)(2,1)S(1)} %pad_maximum_fusion.refs_0_), channel_id=1, source_target_pairs={{0,4},{4,8},{8,12},{12,16},{16,20},{20,24},{24,28},{1,5},{5,9},{9,... | collective-permute-start | bytes 393224 | tf_op jit(solution)/shard_map/ppermute | solution.py:258
  8.1 5.1 %collective-permute-start.4 = (bf16[256,256]{1,0:T(8,128)(2,1)S(1)}, bf16[256,256]{1,0:T(8,128)(2,1)S(1)}, u32[]{:S(2)}, u32[]{:S(2)}) collective-permute-start(bf16[256,256]{1,0:T(8,128)(2,1)S(1)} %pad_maximum_fusion.refs_0_), channel_id=1, source_target_pairs={{0,12},{4,16},{8,20},{12,24},{16,28},{1,13},{5,17},{9,21},{13,25},... | collective-permute-start | bytes 393224 | tf_op jit(solution)/shard_map/ppermute | solution.py:258
  13.2 2.7 %collective-permute-start.3 = (bf16[256,256]{1,0:T(8,128)(2,1)S(1)}, bf16[256,256]{1,0:T(8,128)(2,1)S(1)}, u32[]{:S(2)}, u32[]{:S(2)}) collective-permute-start(bf16[256,256]{1,0:T(8,128)(2,1)S(1)} %pad_maximum_fusion.refs_0_), channel_id=1, source_target_pairs={{0,8},{4,12},{8,16},{12,20},{16,24},{20,28},{1,9},{5,13},{9,17},{1... | collective-permute-start | bytes 393224 | tf_op jit(solution)/shard_map/ppermute | solution.py:258
  16.0 1.3 %collective-permute-start.7 = (bf16[256,256]{1,0:T(8,128)(2,1)S(1)}, bf16[256,256]{1,0:T(8,128)(2,1)S(1)}, u32[]{:S(2)}, u32[]{:S(2)}) collective-permute-start(bf16[256,256]{1,0:T(8,128)(2,1)S(1)} %pad_maximum_fusion.refs_0_), channel_id=1, source_target_pairs={{0,20},{4,24},{8,28},{1,21},{5,25},{9,29},{2,22},{6,26},{10,30},{3... | collective-permute-start | bytes 393224 | tf_op jit(solution)/shard_map/ppermute | solution.py:258
  17.3 1.7 %collective-permute-start.6 = (bf16[256,256]{1,0:T(8,128)(2,1)S(1)}, bf16[256,256]{1,0:T(8,128)(2,1)S(1)}, u32[]{:S(2)}, u32[]{:S(2)}) collective-permute-start(bf16[256,256]{1,0:T(8,128)(2,1)S(1)} %pad_maximum_fusion.refs_0_), channel_id=1, source_target_pairs={{0,16},{4,20},{8,24},{12,28},{1,17},{5,21},{9,25},{13,29},{2,18},{... | collective-permute-start | bytes 393224 | tf_op jit(solution)/shard_map/ppermute | solution.py:258
  19.0 1.0 %copy.10 = bf16[4,256,128]{2,1,0:T(8,128)(2,1)S(1)} copy(bf16[4,256,128]{2,0,1:T(4,128)(2,1)} %bitcast.14) | data formatting | bytes 524288 | tf_op jit(solution)/shard_map/transpose | solution.py:268
  20.0 0.6 %copy-done.2 = s32[16]{0:T(128)S(1)} copy-done((s32[16]{0:T(128)S(1)}, s32[16]{0:T(128)}, u32[]{:S(2)}) %copy-start.2) | copy-done | bytes 88
  20.6 0.6 %begin.1.begin_ref = s32[1,256]{1,0:T(1,128)S(1)} custom-call(s32[16]{0:T(128)S(1)} %copy-done.2), custom_call_target="tpu_custom_call" | custom-call | flops 200000000 | tf_op jit(solution)/shard_map/begin/pallas_call | solution.py:226
  21.3 1.3 %forward_near.1 = (f32[1,1024]{1,0:T(1,128)S(1)}, f32[1,1024]{1,0:T(1,128)S(1)}, f32[128,1024]{1,0:T(8,128)S(1)}) custom-call(s32[16]{0:T(128)S(1)} %copy-done.2, s32[1,256]{1,0:T(1,128)S(1)} %begin.1.begin_ref, bf16[1024,128]{1,0:T(8,128)(2,1)S(1)} %bitcast.7, bf16[256,256]{1,0:T(8,128)(2,1)S(1)} %pad_maximum_fusion.refs_0_, ...), custom_call_target="tpu_custom_call" | custom-call | flops 6000000000 | tf_op jit(solution)/shard_map/forward_near/pallas_call | solution.py:226
  22.6 0.6 %collective-permute-done.5.diag_ref = bf16[64,4096]{1,0:T(8,128)(2,1)S(1)} collective-permute-done((bf16[64,4096]{1,0:T(8,128)(2,1)S(1)}, bf16[64,4096]{1,0:T(8,128)(2,1)S(1)}, u32[]{:S(2)}, u32[]{:S(2)}) %collective-permute-start.5) | collective-permute-done | bytes 524320 | tf_op jit(solution)/shard_map/ppermute | solution.py:254
  23.6 1.4 %d_attn.1.g_ref.refs_3_.refs_2_.refs_1_ = bf16[1024,128]{1,0:T(8,128)(2,1)S(1)} custom-call(bf16[64,4096]{1,0:T(8,128)(2,1)S(1)} %copy-done.1, bf16[64,4096]{1,0:T(8,128)(2,1)S(1)} %collective-permute-done.pair_ref, bf16[64,4096]{1,0:T(8,128)(2,1)S(1)} %collective-permute-done.2.cross_ref, bf16[64,4096]{1,0:T(8,128)(2,1)S(1)} %collective-permute-done.5.diag_ref, ...), custom_call_target="tpu_custom_call" | custom-call | flops 2000000000 | tf_op jit(solution)/shard_map/d_attn/pallas_call | solution.py:226
  25.0 0.7 %forward_far.1 = (bf16[256,512]{1,0:T(8,128)(2,1)S(1)}, f32[1,1024]{1,0:T(1,128)S(1)}) custom-call(s32[16]{0:T(128)S(1)} %copy-done.2, s32[1,256]{1,0:T(1,128)S(1)} %begin.1.begin_ref, bf16[1024,128]{1,0:T(8,128)(2,1)S(1)} %bitcast.8, bf16[256,256]{1,0:T(8,128)(2,1)S(1)} %collective-permute-done.6.refs_0_.refs_1_, ...), custom_call_target="tpu_custom_call" | custom-call | flops 5000000000 | tf_op jit(solution)/shard_map/forward_far/pallas_call | solution.py:226
  25.8 1.3 %project.1 = (bf16[128,4096]{1,0:T(8,128)(2,1)S(1)}, bf16[128,4096]{1,0:T(8,128)(2,1)S(1)}, f32[1,1024]{1,0:T(1,128)S(1)}) custom-call(bf16[256,512]{1,0:T(8,128)(2,1)S(1)} %get-tuple-element.64.attn_ref, bf16[1024,128]{1,0:T(8,128)(2,1)S(1)} %d_attn.1.g_ref.refs_3_.refs_2_.refs_1_, bf16[512,4096]{1,0:T(8,128)(2,1)S(1)} %bitcast.13), custom_call_target="tpu_custom_call" | custom-call | flops 2000000000 | tf_op jit(solution)/shard_map/project/pallas_call | solution.py:226
  27.6 1.3 %backward_first.1 = (f32[128,1024]{1,0:T(8,128)S(1)}, bf16[256,256]{1,0:T(8,128)(2,1)}, bf16[256,256]{1,0:T(8,128)(2,1)S(1)}, bf16[256,256]{1,0:T(8,128)(2,1)S(1)}) custom-call(s32[16]{0:T(128)S(1)} %copy-done.3, s32[1,256]{1,0:T(1,128)S(1)} %begin.1.begin_ref, bf16[1024,128]{1,0:T(8,128)(2,1)S(1)} %bitcast.9, ...), custom_call_target="tpu_custom_call" | custom-call | flops 3000000000 | tf_op jit(solution)/shard_map/backward_first/pallas_call | solution.py:226
  28.9 1.0 %collective-permute-done.8.pair_ref = bf16[128,4096]{1,0:T(8,128)(2,1)S(1)} collective-permute-done((bf16[128,4096]{1,0:T(8,128)(2,1)S(1)}, bf16[128,4096]{1,0:T(8,128)(2,1)S(1)}, u32[]{:S(2)}, u32[]{:S(2)}) %collective-permute-start.8) | collective-permute-done | bytes 1048608 | tf_op jit(solution)/shard_map/ppermute | solution.py:254
  30.0 0.6 %collective-permute-start.9 = (bf16[64,4096]{1,0:T(8,128)(2,1)S(1)}, bf16[64,4096]{1,0:T(8,128)(2,1)S(1)}, u32[]{:S(2)}, u32[]{:S(2)}) collective-permute-start(bf16[64,4096]{1,0:T(8,128)(2,1)S(1)} %pair_sum.1), channel_id=1, source_target_pairs={{0,2},{1,3},{2,0},{3,1},{4,6},{5,7},{6,4},{7,5},{8,10},{9,11},{10,... | collective-permute-start | bytes 1572872 | tf_op jit(solution)/shard_map/ppermute | solution.py:254
  30.6 1.3 %collective-permute-start.10 = (bf16[256,256]{1,0:T(8,128)(2,1)S(1)}, bf16[256,256]{1,0:T(8,128)(2,1)S(1)}, u32[]{:S(2)}, u32[]{:S(2)}) collective-permute-start(bf16[256,256]{1,0:T(8,128)(2,1)S(1)} %get-tuple-element.78), channel_id=1, source_target_pairs={{20,0},{24,4},{28,8},{21,1},{25,5},{29,9},{22,2},{26,6},{30,10},{2... | collective-permute-start | bytes 393224 | tf_op jit(solution)/shard_map/ppermute | solution.py:258
  31.9 1.3 %collective-permute-start.12 = (bf16[256,256]{1,0:T(8,128)(2,1)}, bf16[256,256]{1,0:T(8,128)(2,1)}, u32[]{:S(2)}, u32[]{:S(2)}) collective-permute-start(bf16[256,256]{1,0:T(8,128)(2,1)} %get-tuple-element.80), channel_id=1, source_target_pairs={{8,0},{12,4},{16,8},{20,12},{24,16},{28,20},{9,1},{13,5},{17,9},{2... | collective-permute-start | bytes 393224 | tf_op jit(solution)/shard_map/ppermute | solution.py:258
  33.2 1.3 %collective-permute-start.13 = (bf16[256,256]{1,0:T(8,128)(2,1)S(1)}, bf16[256,256]{1,0:T(8,128)(2,1)}, u32[]{:S(2)}, u32[]{:S(2)}) collective-permute-start(bf16[256,256]{1,0:T(8,128)(2,1)S(1)} %get-tuple-element.81), channel_id=1, source_target_pairs={{12,0},{16,4},{20,8},{24,12},{28,16},{13,1},{17,5},{21,9},{25,13},... | collective-permute-start | bytes 393224 | tf_op jit(solution)/shard_map/ppermute | solution.py:258
  34.5 1.3 %backward_second.1 = (f32[128,1024]{1,0:T(8,128)S(1)}, bf16[256,256]{1,0:T(8,128)(2,1)}, bf16[256,256]{1,0:T(8,128)(2,1)}) custom-call(s32[16]{0:T(128)S(1)} %copy-done.3, s32[1,256]{1,0:T(1,128)S(1)} %begin.1.begin_ref, bf16[1024,128]{1,0:T(8,128)(2,1)S(1)} %bitcast.10, bf16[256,256]{1,0:T(8,128)(2,1)S(1)} %collective-permute-done.1.refs_1_.refs_0_, ...), custom_call_target="tpu_custom_call" | custom-call | flops 3000000000 | tf_op jit(solution)/shard_map/backward_second/pallas_call | solution.py:226
  35.9 5.3 %collective-permute-done.10.refs_5_ = bf16[256,256]{1,0:T(8,128)(2,1)S(1)} collective-permute-done((bf16[256,256]{1,0:T(8,128)(2,1)S(1)}, bf16[256,256]{1,0:T(8,128)(2,1)S(1)}, u32[]{:S(2)}, u32[]{:S(2)}) %collective-permute-start.10) | collective-permute-done | bytes 131104 | tf_op jit(solution)/shard_map/ppermute | solution.py:258
  41.1 1.3 %collective-permute-start.11 = (bf16[256,256]{1,0:T(8,128)(2,1)}, bf16[256,256]{1,0:T(8,128)(2,1)}, u32[]{:S(2)}, u32[]{:S(2)}) collective-permute-start(bf16[256,256]{1,0:T(8,128)(2,1)} %get-tuple-element.79), channel_id=1, source_target_pairs={{4,0},{8,4},{12,8},{16,12},{20,16},{24,20},{28,24},{5,1},{9,5},{13... | collective-permute-start | bytes 393224 | tf_op jit(solution)/shard_map/ppermute | solution.py:258
  42.4 1.3 %collective-permute-start.14 = (bf16[256,256]{1,0:T(8,128)(2,1)}, bf16[256,256]{1,0:T(8,128)(2,1)}, u32[]{:S(2)}, u32[]{:S(2)}) collective-permute-start(bf16[256,256]{1,0:T(8,128)(2,1)} %get-tuple-element.82), channel_id=1, source_target_pairs={{16,0},{20,4},{24,8},{28,12},{17,1},{21,5},{25,9},{29,13},{18,2},{... | collective-permute-start | bytes 393224 | tf_op jit(solution)/shard_map/ppermute | solution.py:258
  43.7 1.5 %backward_own.1 = (bf16[256,512]{1,0:T(8,128)(2,1)S(1)}, bf16[256,256]{1,0:T(8,128)(2,1)S(1)}) custom-call(s32[16]{0:T(128)S(1)} %copy-done.3, s32[1,256]{1,0:T(1,128)S(1)} %begin.1.begin_ref, bf16[1024,128]{1,0:T(8,128)(2,1)S(1)} %bitcast.11, bf16[256,256]{1,0:T(8,128)(2,1)S(1)} %pad_maximum_fusion.refs_0_, ...), custom_call_target="tpu_custom_call" | custom-call | flops 2000000000 | tf_op jit(solution)/shard_map/backward_own/pallas_call | solution.py:226
  45.3 0.6 %copy-done.4 = bf16[256,256]{1,0:T(8,128)(2,1)} copy-done((bf16[256,256]{1,0:T(8,128)(2,1)}, bf16[256,256]{1,0:T(8,128)(2,1)S(1)}, u32[]{:S(2)}) %copy-start.4) | copy-done | bytes 131096
  45.9 0.8 %reshape.33 = bf16[256,4,128]{2,1,0:T(4,128)(2,1)} reshape(bf16[256,512]{1,0:T(8,128)(2,1)S(1)} %get-tuple-element.75) | data formatting | bytes 524288 | tf_op jit(solution)/shard_map/reshape | solution.py:357
  46.7 1.0 %mixed_sum.1 = bf16[64,4096]{1,0:T(8,128)(2,1)} custom-call(bf16[128,4096]{1,0:T(8,128)(2,1)S(1)} %get-tuple-element.69.keep_ref, bf16[128,4096]{1,0:T(8,128)(2,1)S(1)} %collective-permute-done.8.pair_ref, bf16[64,4096]{1,0:T(8,128)(2,1)S(1)} %collective-permute-done.9.cross_ref), custom_call_target="tpu_custom_call" | custom-call | flops 500000000 | tf_op jit(solution)/shard_map/mixed_sum/pallas_call | solution.py:226
  47.7 1.3 %collective-permute-done.11.refs_1_ = bf16[256,256]{1,0:T(8,128)(2,1)} collective-permute-done((bf16[256,256]{1,0:T(8,128)(2,1)}, bf16[256,256]{1,0:T(8,128)(2,1)}, u32[]{:S(2)}, u32[]{:S(2)}) %collective-permute-start.11) | collective-permute-done | bytes 131104 | tf_op jit(solution)/shard_map/ppermute | solution.py:258
  49.0 2.7 %collective-permute-done.14.refs_4_ = bf16[256,256]{1,0:T(8,128)(2,1)} collective-permute-done((bf16[256,256]{1,0:T(8,128)(2,1)}, bf16[256,256]{1,0:T(8,128)(2,1)}, u32[]{:S(2)}, u32[]{:S(2)}) %collective-permute-start.14) | collective-permute-done | bytes 131104 | tf_op jit(solution)/shard_map/ppermute | solution.py:258
  51.7 2.0 %finish.1 = (bf16[256,128]{1,0:T(8,128)(2,1)}, bf16[256,128]{1,0:T(8,128)(2,1)}) custom-call(bf16[256,256]{1,0:T(8,128)(2,1)} %copy-done.4, bf16[256,256]{1,0:T(8,128)(2,1)} %collective-permute-done.11.refs_1_, bf16[256,256]{1,0:T(8,128)(2,1)} %collective-permute-done.12.refs_2_, bf16[256,256]{1,0:T(8,128)(2,1)} %collective-permute-done.13.refs_3_, ...), custom_call_target="tpu_custom_call" | custom-call | flops 500000000 | tf_op jit(solution)/shard_map/finish/pallas_call | solution.py:226
  (24 shorter events, 1.7 us)
Async XLA Ops:
  0.6 15.3 %collective-permute-start = (bf16[64,4096]{1,0:T(8,128)(2,1)}, bf16[64,4096]{1,0:T(8,128)(2,1)S(1)}, u32[]{:S(2)}, u32[]{:S(2)}) collective-permute-start(bf16[64,4096]{1,0:T(8,128)(2,1)} %own_ref), channel_id=1, source_target_pairs={{0,1},{1,0},{2,3},{3,2},{4,5},{5,4},{6,7},{7,6},{8,9},{9,8},{10,11... | collective-permute-start | bytes 1572872 | tf_op jit(solution)/shard_map/ppermute | solution.py:254
  1.1 20.0 %collective-permute-start.2 = (bf16[64,4096]{1,0:T(8,128)(2,1)}, bf16[64,4096]{1,0:T(8,128)(2,1)S(1)}, u32[]{:S(2)}, u32[]{:S(2)}) collective-permute-start(bf16[64,4096]{1,0:T(8,128)(2,1)} %own_ref), channel_id=1, source_target_pairs={{0,2},{1,3},{2,0},{3,1},{4,6},{5,7},{6,4},{7,5},{8,10},{9,11},{10,... | collective-permute-start | bytes 1572872 | tf_op jit(solution)/shard_map/ppermute | solution.py:254
  4.6 11.3 %collective-permute-start.1 = (bf16[256,256]{1,0:T(8,128)(2,1)S(1)}, bf16[256,256]{1,0:T(8,128)(2,1)S(1)}, u32[]{:S(2)}, u32[]{:S(2)}) collective-permute-start(bf16[256,256]{1,0:T(8,128)(2,1)S(1)} %pad_maximum_fusion.refs_0_), channel_id=1, source_target_pairs={{0,4},{4,8},{8,12},{12,16},{16,20},{20,24},{24,28},{1,5},{5,9},{9,... | collective-permute-start | bytes 393224 | tf_op jit(solution)/shard_map/ppermute | solution.py:258
  8.1 13.2 %collective-permute-start.4 = (bf16[256,256]{1,0:T(8,128)(2,1)S(1)}, bf16[256,256]{1,0:T(8,128)(2,1)S(1)}, u32[]{:S(2)}, u32[]{:S(2)}) collective-permute-start(bf16[256,256]{1,0:T(8,128)(2,1)S(1)} %pad_maximum_fusion.refs_0_), channel_id=1, source_target_pairs={{0,12},{4,16},{8,20},{12,24},{16,28},{1,13},{5,17},{9,21},{13,25},... | collective-permute-start | bytes 393224 | tf_op jit(solution)/shard_map/ppermute | solution.py:258
  13.2 8.1 %collective-permute-start.3 = (bf16[256,256]{1,0:T(8,128)(2,1)S(1)}, bf16[256,256]{1,0:T(8,128)(2,1)S(1)}, u32[]{:S(2)}, u32[]{:S(2)}) collective-permute-start(bf16[256,256]{1,0:T(8,128)(2,1)S(1)} %pad_maximum_fusion.refs_0_), channel_id=1, source_target_pairs={{0,8},{4,12},{8,16},{12,20},{16,24},{20,28},{1,9},{5,13},{9,17},{1... | collective-permute-start | bytes 393224 | tf_op jit(solution)/shard_map/ppermute | solution.py:258
  16.0 9.0 %collective-permute-start.7 = (bf16[256,256]{1,0:T(8,128)(2,1)S(1)}, bf16[256,256]{1,0:T(8,128)(2,1)S(1)}, u32[]{:S(2)}, u32[]{:S(2)}) collective-permute-start(bf16[256,256]{1,0:T(8,128)(2,1)S(1)} %pad_maximum_fusion.refs_0_), channel_id=1, source_target_pairs={{0,20},{4,24},{8,28},{1,21},{5,25},{9,29},{2,22},{6,26},{10,30},{3... | collective-permute-start | bytes 393224 | tf_op jit(solution)/shard_map/ppermute | solution.py:258
  17.3 7.7 %collective-permute-start.6 = (bf16[256,256]{1,0:T(8,128)(2,1)S(1)}, bf16[256,256]{1,0:T(8,128)(2,1)S(1)}, u32[]{:S(2)}, u32[]{:S(2)}) collective-permute-start(bf16[256,256]{1,0:T(8,128)(2,1)S(1)} %pad_maximum_fusion.refs_0_), channel_id=1, source_target_pairs={{0,16},{4,20},{8,24},{12,28},{1,17},{5,21},{9,25},{13,29},{2,18},{... | collective-permute-start | bytes 393224 | tf_op jit(solution)/shard_map/ppermute | solution.py:258
  20.0 0.7 %copy-start.2 = (s32[16]{0:T(128)S(1)}, s32[16]{0:T(128)}, u32[]{:S(2)}) copy-start(s32[16]{0:T(128)} %len_ref.5) | copy-start | bytes 196
  21.2 2.0 %collective-permute-start.5 = (bf16[64,4096]{1,0:T(8,128)(2,1)S(1)}, bf16[64,4096]{1,0:T(8,128)(2,1)S(1)}, u32[]{:S(2)}, u32[]{:S(2)}) collective-permute-start(bf16[64,4096]{1,0:T(8,128)(2,1)S(1)} %collective-permute-done.2.cross_ref), channel_id=1, source_target_pairs={{0,1},{1,0},{2,3},{3,2},{4,5},{5,4},{6,7},{7,6},{8,9},{9,8},{10,11... | collective-permute-start | bytes 1572872 | tf_op jit(solution)/shard_map/ppermute | solution.py:254
  21.3 2.2 %copy-start = (bf16[4,128,4096]{2,1,0:T(8,128)(2,1)S(1)}, bf16[4,128,4096]{2,1,0:T(8,128)(2,1)}, u32[]{:S(2)}) copy-start(bf16[4,128,4096]{2,1,0:T(8,128)(2,1)} %param.9) | copy-start | bytes 12582916
  21.3 2.3 %copy-start.1 = (bf16[64,4096]{1,0:T(8,128)(2,1)S(1)}, bf16[64,4096]{1,0:T(8,128)(2,1)}, u32[]{:S(2)}) copy-start(bf16[64,4096]{1,0:T(8,128)(2,1)} %own_ref) | copy-start | bytes 1572868
  25.8 1.9 %copy-start.3 = (s32[16]{0:T(128)S(1)}, s32[16]{0:T(128)}, u32[]{:S(2)}) copy-start(s32[16]{0:T(128)} %len_ref.5) | copy-start | bytes 196
  27.1 2.8 %collective-permute-start.8 = (bf16[128,4096]{1,0:T(8,128)(2,1)S(1)}, bf16[128,4096]{1,0:T(8,128)(2,1)S(1)}, u32[]{:S(2)}, u32[]{:S(2)}) collective-permute-start(bf16[128,4096]{1,0:T(8,128)(2,1)S(1)} %get-tuple-element.66), channel_id=1, source_target_pairs={{0,1},{1,0},{2,3},{3,2},{4,5},{5,4},{6,7},{7,6},{8,9},{9,8},{10,11... | collective-permute-start | bytes 3145736 | tf_op jit(solution)/shard_map/ppermute | solution.py:254
  30.0 16.6 %collective-permute-start.9 = (bf16[64,4096]{1,0:T(8,128)(2,1)S(1)}, bf16[64,4096]{1,0:T(8,128)(2,1)S(1)}, u32[]{:S(2)}, u32[]{:S(2)}) collective-permute-start(bf16[64,4096]{1,0:T(8,128)(2,1)S(1)} %pair_sum.1), channel_id=1, source_target_pairs={{0,2},{1,3},{2,0},{3,1},{4,6},{5,7},{6,4},{7,5},{8,10},{9,11},{10,... | collective-permute-start | bytes 1572872 | tf_op jit(solution)/shard_map/ppermute | solution.py:254
  30.6 10.5 %collective-permute-start.10 = (bf16[256,256]{1,0:T(8,128)(2,1)S(1)}, bf16[256,256]{1,0:T(8,128)(2,1)S(1)}, u32[]{:S(2)}, u32[]{:S(2)}) collective-permute-start(bf16[256,256]{1,0:T(8,128)(2,1)S(1)} %get-tuple-element.78), channel_id=1, source_target_pairs={{20,0},{24,4},{28,8},{21,1},{25,5},{29,9},{22,2},{26,6},{30,10},{2... | collective-permute-start | bytes 393224 | tf_op jit(solution)/shard_map/ppermute | solution.py:258
  31.9 15.7 %collective-permute-start.12 = (bf16[256,256]{1,0:T(8,128)(2,1)}, bf16[256,256]{1,0:T(8,128)(2,1)}, u32[]{:S(2)}, u32[]{:S(2)}) collective-permute-start(bf16[256,256]{1,0:T(8,128)(2,1)} %get-tuple-element.80), channel_id=1, source_target_pairs={{8,0},{12,4},{16,8},{20,12},{24,16},{28,20},{9,1},{13,5},{17,9},{2... | collective-permute-start | bytes 393224 | tf_op jit(solution)/shard_map/ppermute | solution.py:258
  33.2 14.5 %collective-permute-start.13 = (bf16[256,256]{1,0:T(8,128)(2,1)S(1)}, bf16[256,256]{1,0:T(8,128)(2,1)}, u32[]{:S(2)}, u32[]{:S(2)}) collective-permute-start(bf16[256,256]{1,0:T(8,128)(2,1)S(1)} %get-tuple-element.81), channel_id=1, source_target_pairs={{12,0},{16,4},{20,8},{24,12},{28,16},{13,1},{17,5},{21,9},{25,13},... | collective-permute-start | bytes 393224 | tf_op jit(solution)/shard_map/ppermute | solution.py:258
  41.1 2.6 %copy-start.5 = (bf16[256,256]{1,0:T(8,128)(2,1)}, bf16[256,256]{1,0:T(8,128)(2,1)S(1)}, u32[]{:S(2)}) copy-start(bf16[256,256]{1,0:T(8,128)(2,1)S(1)} %collective-permute-done.10.refs_5_) | copy-start | bytes 393220
  41.1 7.8 %collective-permute-start.11 = (bf16[256,256]{1,0:T(8,128)(2,1)}, bf16[256,256]{1,0:T(8,128)(2,1)}, u32[]{:S(2)}, u32[]{:S(2)}) collective-permute-start(bf16[256,256]{1,0:T(8,128)(2,1)} %get-tuple-element.79), channel_id=1, source_target_pairs={{4,0},{8,4},{12,8},{16,12},{20,16},{24,20},{28,24},{5,1},{9,5},{13... | collective-permute-start | bytes 393224 | tf_op jit(solution)/shard_map/ppermute | solution.py:258
  42.4 9.3 %collective-permute-start.14 = (bf16[256,256]{1,0:T(8,128)(2,1)}, bf16[256,256]{1,0:T(8,128)(2,1)}, u32[]{:S(2)}, u32[]{:S(2)}) collective-permute-start(bf16[256,256]{1,0:T(8,128)(2,1)} %get-tuple-element.82), channel_id=1, source_target_pairs={{16,0},{20,4},{24,8},{28,12},{17,1},{21,5},{25,9},{29,13},{18,2},{... | collective-permute-start | bytes 393224 | tf_op jit(solution)/shard_map/ppermute | solution.py:258
  45.3 0.6 %copy-start.4 = (bf16[256,256]{1,0:T(8,128)(2,1)}, bf16[256,256]{1,0:T(8,128)(2,1)S(1)}, u32[]{:S(2)}) copy-start(bf16[256,256]{1,0:T(8,128)(2,1)S(1)} %get-tuple-element.76.refs_0_) | copy-start | bytes 393220
